TPU v7x, 512 devices: a whole 4x8x8 slice. The times are simulated.
512 devices in a mesh: dp: 16 (over y, core), ctx: 32 (over x, z).
Axes of the slice: x: 4, y: 8, z: 8, core: 2. Of those that a mesh axis runs over, the one named last changes fastest.
Arguments:
- queries: bfloat16 [16, 4096, 4096], P('dp', 'ctx'), may hold values from -45 to 45
- key_head_states: bfloat16 [16, 4096, 512], P('dp', 'ctx'), may hold values from -6 to 6
- value_head_states: bfloat16 [16, 4096, 512], P('dp', 'ctx'), may hold values from -6 to 6
- out_grad: bfloat16 [16, 4096, 4096], P('dp', 'ctx'), may hold values from -24 to 24
- doc_blocks: int32 [16, 21], P('dp'), may hold values from 1 to 8, as said below
- block_order: int32 [16, 64], P('dp'), may hold values from 0 to 63, as said below
- target_mask: int32 [16, 4096], P('dp', 'ctx'), may hold values from 0 to 1, as said below
Outputs:
- attended: bfloat16 [16, 4096, 4096], P('dp', 'ctx')
- grad_queries: bfloat16 [16, 4096, 4096], P('dp', 'ctx')
- grad_keys: bfloat16 [16, 4096, 512], P('dp', 'ctx')
- grad_values: bfloat16 [16, 4096, 512], P('dp', 'ctx')
Inputs may be any that keep to these rules, and one draw needn't show every extreme that they name: `doc_blocks`: each pack's lengths sum to 64; the longest is 8. `block_order`: each pack's row is a permutation of its blocks that stores the blocks of every document next to one another and in pack order. `target_mask`: the first token of every stored block is 1.
All inputs are finite; a program needn't handle non-finite values.
Results may differ from a plain program's by a relative error of at most 0.03.
Values may be sent and summed in bfloat16 or wider, within the bound.
No kernel may reach another device: no remote copies, remote signals or barrier semaphores. Data moves between devices by JAX's collectives and lax.ppermute only.
A program may use at most 64 MiB of HBM per device.

v0:
```python
import math

import jax
import jax.numpy as jnp
from jax import lax
from jax.sharding import PartitionSpec as P

HEAD_WIDTH = 128
QUERY_HEADS = 32
KEY_VALUE_HEADS = 4
ALIGN_TOKENS = 64
MOST = 8


def block_documents(doc_lengths, block_count, block_size):
    ends = jnp.cumsum(doc_lengths, dtype=jnp.int32)
    block_ids = jnp.arange(block_count, dtype=jnp.int32)
    owners = jnp.sum((block_ids[:, None] >= ends[None, :]).astype(jnp.int32), axis=1)
    return jnp.repeat(owners, block_size)


def token_permute(stored, positions, block_size):
    pieces = stored.reshape((stored.shape[0] // block_size, block_size) + stored.shape[1:])
    return jnp.take(pieces, positions, axis=0).reshape(stored.shape)


def band_pass(queries, key_head_states, value_head_states, grads, documents, span):
    pack_rows, head_count, head_size = queries.shape
    inv_scale = 1.0 / math.sqrt(head_size)
    row_numbers = jnp.arange(span, dtype=jnp.int32)
    col_ids = jnp.arange(2 * span, dtype=jnp.int32)

    def step(carry, step_index):
        acc_keys, acc_values = carry
        q_start = step_index * span
        k_start = jnp.maximum(step_index - 1, 0) * span
        q_block = lax.dynamic_slice_in_dim(queries, q_start, span, 0)
        g_block = lax.dynamic_slice_in_dim(grads, q_start, span, 0)
        k_window = lax.dynamic_slice_in_dim(key_head_states, k_start, 2 * span, 0)
        v_window = lax.dynamic_slice_in_dim(value_head_states, k_start, 2 * span, 0)
        q_docs = lax.dynamic_slice_in_dim(documents, q_start, span, 0)
        k_docs = lax.dynamic_slice_in_dim(documents, k_start, 2 * span, 0)
        visible = (q_docs[:, None] == k_docs[None, :]) & (
            k_start + col_ids[None, :] <= q_start + row_numbers[:, None]
        )
        scores = (
            jnp.einsum("qhd,khd->hqk", q_block, k_window, preferred_element_type=jnp.float32)
            * inv_scale
        )
        scores = jnp.where(visible[None], scores, -1e30)
        peak = jnp.max(scores, axis=2, keepdims=True)
        expo = jnp.exp(scores - peak)
        prob_high = expo / jnp.sum(expo, axis=2, keepdims=True)
        prob_low = prob_high.astype(jnp.bfloat16)
        out_block = jnp.einsum(
            "hqk,khd->qhd", prob_low, v_window, preferred_element_type=jnp.float32
        ).astype(jnp.bfloat16)
        delta = jnp.sum(g_block.astype(jnp.float32) * out_block.astype(jnp.float32), axis=2)
        dprob = jnp.einsum("qhd,khd->hqk", g_block, v_window, preferred_element_type=jnp.float32)
        dscore = (prob_high * (dprob - jnp.transpose(delta)[:, :, None]) * inv_scale).astype(
            jnp.bfloat16
        )
        dq_block = jnp.einsum(
            "hqk,khd->qhd", dscore, k_window, preferred_element_type=jnp.float32
        ).astype(jnp.bfloat16)
        key_part = jnp.einsum("hqk,qhd->khd", dscore, q_block, preferred_element_type=jnp.float32)
        value_part = jnp.einsum(
            "hqk,qhd->khd", prob_low, g_block, preferred_element_type=jnp.float32
        )
        acc_keys = lax.dynamic_update_slice_in_dim(
            acc_keys,
            lax.dynamic_slice_in_dim(acc_keys, k_start, 2 * span, 0) + key_part,
            k_start,
            0,
        )
        acc_values = lax.dynamic_update_slice_in_dim(
            acc_values,
            lax.dynamic_slice_in_dim(acc_values, k_start, 2 * span, 0) + value_part,
            k_start,
            0,
        )
        return ((acc_keys, acc_values), (out_block, dq_block))

    zeros_acc = jnp.zeros((pack_rows, head_count, head_size), jnp.float32)
    (acc_keys, acc_values), (out_blocks, dq_blocks) = lax.scan(
        step, (zeros_acc, zeros_acc), jnp.arange(pack_rows // span, dtype=jnp.int32)
    )
    attention_output = out_blocks.reshape(pack_rows, head_count, head_size)
    query_gradient = dq_blocks.reshape(pack_rows, head_count, head_size)
    return (attention_output, query_gradient, acc_keys, acc_values)


def shards(
    queries, key_head_states, value_head_states, out_grad, doc_blocks, block_order, target_mask
):
    token_rows = queries.shape[1]
    ctx_count = lax.axis_size("ctx")
    pack_rows = token_rows * ctx_count
    head_count = QUERY_HEADS // ctx_count
    query_per_group = QUERY_HEADS // KEY_VALUE_HEADS
    block_count = pack_rows // ALIGN_TOKENS
    span = MOST * ALIGN_TOKENS
    local_count = jnp.sum(target_mask.astype(jnp.float32))
    target_total = lax.psum(local_count, ("dp", "ctx"))
    factor = lax.axis_size("dp") * pack_rows / target_total
    grads = (
        out_grad.astype(jnp.float32) * (target_mask.astype(jnp.float32)[:, :, None] * factor)
    ).astype(jnp.bfloat16)
    spread_keys = jnp.broadcast_to(
        key_head_states.reshape(1, token_rows, KEY_VALUE_HEADS, 1, HEAD_WIDTH),
        (1, token_rows, KEY_VALUE_HEADS, query_per_group, HEAD_WIDTH),
    ).reshape(1, token_rows, QUERY_HEADS * HEAD_WIDTH)
    spread_values = jnp.broadcast_to(
        value_head_states.reshape(1, token_rows, KEY_VALUE_HEADS, 1, HEAD_WIDTH),
        (1, token_rows, KEY_VALUE_HEADS, query_per_group, HEAD_WIDTH),
    ).reshape(1, token_rows, QUERY_HEADS * HEAD_WIDTH)
    head_queries, head_grads, head_keys, head_values = (
        lax.all_to_all(queries, "ctx", split_axis=2, concat_axis=1, tiled=True),
        lax.all_to_all(grads, "ctx", split_axis=2, concat_axis=1, tiled=True),
        lax.all_to_all(spread_keys, "ctx", split_axis=2, concat_axis=1, tiled=True),
        lax.all_to_all(spread_values, "ctx", split_axis=2, concat_axis=1, tiled=True),
    )
    positioned = block_order[0]
    inverse_permute = (
        jnp.zeros((block_count,), jnp.int32)
        .at[positioned]
        .set(jnp.arange(block_count, dtype=jnp.int32))
    )
    documents = block_documents(doc_blocks[0], block_count, ALIGN_TOKENS)
    q_true = token_permute(
        head_queries.reshape(pack_rows, head_count, HEAD_WIDTH), inverse_permute, ALIGN_TOKENS
    )
    g_true = token_permute(
        head_grads.reshape(pack_rows, head_count, HEAD_WIDTH), inverse_permute, ALIGN_TOKENS
    )
    exact_keys = token_permute(
        head_keys.reshape(pack_rows, head_count, HEAD_WIDTH), inverse_permute, ALIGN_TOKENS
    )
    exact_values = token_permute(
        head_values.reshape(pack_rows, head_count, HEAD_WIDTH), inverse_permute, ALIGN_TOKENS
    )
    attention_output, query_gradient, key_gradient_terms, value_gradient_terms = band_pass(
        q_true, exact_keys, exact_values, g_true, documents, span
    )
    out_stored = token_permute(attention_output, positioned, ALIGN_TOKENS).reshape(
        1, pack_rows, head_count * HEAD_WIDTH
    )
    dq_stored = token_permute(query_gradient, positioned, ALIGN_TOKENS).reshape(
        1, pack_rows, head_count * HEAD_WIDTH
    )
    dk_stored = token_permute(key_gradient_terms, positioned, ALIGN_TOKENS).reshape(
        1, pack_rows, head_count * HEAD_WIDTH
    )
    dv_stored = token_permute(value_gradient_terms, positioned, ALIGN_TOKENS).reshape(
        1, pack_rows, head_count * HEAD_WIDTH
    )
    attended, grad_queries = (
        lax.all_to_all(out_stored, "ctx", split_axis=1, concat_axis=2, tiled=True),
        lax.all_to_all(dq_stored, "ctx", split_axis=1, concat_axis=2, tiled=True),
    )
    returned_keys, returned_values = (
        lax.all_to_all(dk_stored, "ctx", split_axis=1, concat_axis=2, tiled=True),
        lax.all_to_all(dv_stored, "ctx", split_axis=1, concat_axis=2, tiled=True),
    )
    grad_keys = (
        jnp.sum(
            returned_keys.reshape(1, token_rows, KEY_VALUE_HEADS, query_per_group, HEAD_WIDTH),
            axis=3,
        )
        .astype(jnp.bfloat16)
        .reshape(1, token_rows, KEY_VALUE_HEADS * HEAD_WIDTH)
    )
    grad_values = (
        jnp.sum(
            returned_values.reshape(1, token_rows, KEY_VALUE_HEADS, query_per_group, HEAD_WIDTH),
            axis=3,
        )
        .astype(jnp.bfloat16)
        .reshape(1, token_rows, KEY_VALUE_HEADS * HEAD_WIDTH)
    )
    return (attended, grad_queries, grad_keys, grad_values)


def solution(mesh):
    placed = (
        P("dp", "ctx", None),
        P("dp", "ctx", None),
        P("dp", "ctx", None),
        P("dp", "ctx", None),
        P("dp", None),
        P("dp", None),
        P("dp", "ctx"),
    )
    return jax.shard_map(
        shards,
        mesh=mesh,
        in_specs=placed,
        out_specs=(
            P("dp", "ctx", None),
            P("dp", "ctx", None),
            P("dp", "ctx", None),
            P("dp", "ctx", None),
        ),
        check_vma=False,
    )
```

profile of v0, /device:TPU:1, one launch (start us, length us, event | category | flops | bytes accessed | tf_op | source)
XLA Modules:
  0.0 816.9 jit_solution(13622292076207685674)
XLA Ops:
  1.9 16.7 %copy.170 = bf16[1,128,4096]{1,0,2:T(2,128)(2,1)S(1)} copy(bf16[1,128,4096]{1,2,0:T(8,128)(2,1)S(1)} %bitcast.228) | data formatting | bytes 2097152 | tf_op jit(solution)/shard_map/broadcast_in_dim | solution.py:113
  19.2 22.4 %reduce.17 = bf16[4096,128]{1,0:T(8,128)(2,1)S(1)} reduce(bf16[4096,1,128]{2,1,0:T(2,128)(2,1)S(1)} %bitcast.219, bf16[]{:T(256)} %broadcast.151), dimensions={1}, to_apply=%bitcast.173.reduce_sub_computation | reduce | bytes 2097154
  42.7 14.0 %all-to-all-start.3 = ((bf16[32,2,8192]{2,1,0:T(2,128)(2,1)}), bf16[32,2,8192]{2,1,0:T(2,128)(2,1)S(1)}, u32[]{:S(2)}, u32[]{:S(2)}) async-start(bf16[32,2,8192]{2,1,0:T(2,128)(2,1)} %reshape.435), calls=%async_computation.3 | async-start | bytes 2097152 | tf_op jit(solution)/shard_map/all_to_all | solution.py:121
  57.1 16.7 %copy.171 = bf16[1,128,4096]{1,0,2:T(2,128)(2,1)S(1)} copy(bf16[1,128,4096]{1,2,0:T(8,128)(2,1)S(1)} %bitcast.229) | data formatting | bytes 2097152 | tf_op jit(solution)/shard_map/broadcast_in_dim | solution.py:109
  73.9 23.3 %reduce.18 = bf16[4096,128]{1,0:T(8,128)(2,1)} reduce(bf16[4096,1,128]{2,1,0:T(2,128)(2,1)S(1)} %bitcast.221, bf16[]{:T(256)} %broadcast.151), dimensions={1}, to_apply=%bitcast.174.reduce_sub_computation | reduce | bytes 2097154
  97.2 2.2 reshape.431
  99.5 9.5 %all-to-all-start.1 = ((bf16[32,2,8192]{2,1,0:T(2,128)(2,1)}), bf16[32,2,8192]{2,1,0:T(2,128)(2,1)}, u32[]{:S(2)}, u32[]{:S(2)}) async-start(bf16[32,2,8192]{2,1,0:T(2,128)(2,1)} %reshape.431), calls=%async_computation.1 | async-start | bytes 2097152 | tf_op jit(solution)/shard_map/all_to_all | solution.py:120
  109.6 114.0 %psum.7 = f32[]{:T(128)} all-reduce(f32[]{:T(128)} %convert_reduce_fusion.1), channel_id=1, replica_groups=mesh['dp'=16,'ctx'=32] {'dp','ctx'}, use_global_device_ids=true, to_apply=%region_2.4 | all-reduce | flops 1 | bytes 8 | tf_op jit(solution)/shard_map/psum | solution.py:104
  224.6 2.8 copy.120
  227.4 22.4 %reduce.19 = bf16[4096,128]{1,0:T(8,128)(2,1)S(1)} reduce(bf16[4096,1,128]{2,1,0:T(2,128)(2,1)S(1)} %bitcast.222, bf16[]{:T(256)} %broadcast.151), dimensions={1}, to_apply=%bitcast.151.reduce_sub_computation | reduce | bytes 2097154
  250.9 7.9 all-to-all-start.2
  258.8 2.8 copy.114
  261.6 23.3 %reduce.20 = bf16[4096,128]{1,0:T(8,128)(2,1)} reduce(bf16[4096,1,128]{2,1,0:T(2,128)(2,1)S(1)} %bitcast.224, bf16[]{:T(256)} %broadcast.151), dimensions={1}, to_apply=%bitcast.147.reduce_sub_computation | reduce | bytes 2097154
  285.0 2.3 reshape.429
  287.2 9.5 %all-to-all-start = ((bf16[32,2,8192]{2,1,0:T(2,128)(2,1)}), bf16[32,2,8192]{2,1,0:T(2,128)(2,1)}, u32[]{:S(2)}, u32[]{:S(2)}) async-start(bf16[32,2,8192]{2,1,0:T(2,128)(2,1)} %reshape.429), calls=%async_computation | async-start | bytes 2097152 | tf_op jit(solution)/shard_map/all_to_all | solution.py:118
  302.0 4.3 reshape.432
  310.1 4.3 reshape.434
  318.8 2.6 all-to-all-done
  321.4 4.3 reshape.430
  326.9 2.4 copy.115
  329.3 2.9 gather_fusion
  332.2 3.7 bitcast_select_fusion.4
  339.3 233.1 %while.19 = (s32[]{:T(128)}, f32[4096,1,128]{2,0,1:T(8,128)}, f32[4096,1,128]{2,0,1:T(8,128)}, bf16[8,512,1,128]{3,1,0,2:T(8,128)(2,1)}, bf16[8,512,1,128]{3,1,0...) while((s32[]{:T(128)}, f32[4096,1,128]{2,0,1:T(8,128)}, ...), condition=%wide.region_9.11_spmd.clone, body=%wide.region_5.10_spmd.clone.sunk | while | flops 814350336 | bytes 31896404 | solution.py:85
  348.7 2.1 fusion.63
  356.2 2.1 copy.181
  358.3 2.3 fusion.62
  377.9 2.1 fusion.63
  385.3 2.1 copy.181
  387.4 2.3 fusion.62
  407.0 2.1 fusion.63
  414.4 2.1 copy.181
  416.5 2.3 fusion.62
  436.1 2.1 fusion.63
  443.5 2.1 copy.181
  445.7 2.3 fusion.62
  465.3 2.1 fusion.63
  472.7 2.1 copy.181
  474.8 2.3 fusion.62
  494.4 2.1 fusion.63
  501.8 2.1 copy.181
  503.9 2.3 fusion.62
  523.5 2.1 fusion.63
  531.0 2.1 copy.181
  533.1 2.3 fusion.62
  552.7 2.1 fusion.63
  560.1 2.1 copy.181
  562.2 2.3 fusion.62
  572.5 2.2 gather_fusion.4
  575.8 16.7 %copy.168 = bf16[1,4096,128]{2,0,1:T(2,128)(2,1)S(1)} copy(bf16[1,4096,128]{2,1,0:T(8,128)(2,1)S(1)} %bitcast.227) | data formatting | bytes 2097152 | tf_op jit(solution)/shard_map/reshape;reshape | solution.py:148
  592.5 23.6 %reduce.22 = bf16[4096,128]{1,0:T(8,128)(2,1)} reduce(bf16[4096,1,128]{2,1,0:T(2,128)(2,1)S(1)} %bitcast.223, bf16[]{:T(256)} %broadcast.151), dimensions={1}, to_apply=%bitcast.171.reduce_sub_computation | reduce | bytes 2097154
  616.1 2.1 reshape.439
  618.3 8.6 %all-to-all-start.5 = ((bf16[32,2,8192]{2,1,0:T(2,128)(2,1)}), bf16[32,2,8192]{2,1,0:T(2,128)(2,1)}, u32[]{:S(2)}, u32[]{:S(2)}) async-start(bf16[32,2,8192]{2,1,0:T(2,128)(2,1)} %reshape.439), calls=%async_computation.5 | async-start | bytes 2097152 | tf_op jit(solution)/shard_map/all_to_all | solution.py:159
  626.9 16.7 %copy.169 = bf16[1,4096,128]{2,0,1:T(2,128)(2,1)S(1)} copy(bf16[1,4096,128]{2,1,0:T(8,128)(2,1)S(1)} %bitcast.226) | data formatting | bytes 2097152 | tf_op jit(solution)/shard_map/reshape;reshape | solution.py:145
  643.7 22.4 %reduce.21 = bf16[4096,128]{1,0:T(8,128)(2,1)S(1)} reduce(bf16[4096,1,128]{2,1,0:T(2,128)(2,1)S(1)} %bitcast.220, bf16[]{:T(256)} %broadcast.151), dimensions={1}, to_apply=%bitcast.172.reduce_sub_computation | reduce | bytes 2097154
  667.2 9.2 %all-to-all-start.4 = ((bf16[32,2,8192]{2,1,0:T(2,128)(2,1)}), bf16[32,2,8192]{2,1,0:T(2,128)(2,1)S(1)}, u32[]{:S(2)}, u32[]{:S(2)}) async-start(bf16[32,2,8192]{2,1,0:T(2,128)(2,1)} %reshape.437), calls=%async_computation.4 | async-start | bytes 2097152 | tf_op jit(solution)/shard_map/all_to_all | solution.py:158
  676.3 2.2 gather_fusion.6
  678.5 3.7 gather_fusion.7
  682.2 3.9 bitcast_select_fusion
  686.1 14.7 %all-to-all-done.4 = bf16[32,2,8192]{2,1,0:T(2,128)(2,1)S(1)} async-done(((bf16[32,2,8192]{2,1,0:T(2,128)(2,1)}), bf16[32,2,8192]{2,1,0:T(2,128)(2,1)S(1)}, u32[]{:S(2)}, u32[]{:S(2)}) %all-to-all-start.4) | async-done | bytes 1048608 | tf_op jit(solution)/shard_map/all_to_all | solution.py:158
  700.8 55.2 %all_to_all.126 = f32[1,4096,128]{2,0,1:T(1,128)} all-to-all(f32[1,4096,128]{2,0,1:T(1,128)S(1)} %bitcast.225), channel_id=1, replica_groups=mesh['dp'=16,'ctx'=32] {'ctx'}, dimensions={1} | all-to-all | bytes 4194304 | tf_op jit(solution)/shard_map/all_to_all | solution.py:162
  756.0 8.3 %all-to-all-start.7 = ((f32[1,4096,128]{2,0,1:T(1,128)}), f32[1,4096,128]{2,0,1:T(1,128)}, u32[]{:S(2)}, u32[]{:S(2)}) async-start(f32[1,4096,128]{2,0,1:T(1,128)} %bitcast.54), calls=%async_computation.7 | async-start | bytes 4194304 | tf_op jit(solution)/shard_map/all_to_all | solution.py:163
  764.3 4.3 reshape.440
  775.2 2.3 copy.138
  778.5 35.2 %all-to-all-done.7 = f32[1,4096,128]{2,0,1:T(1,128)} async-done(((f32[1,4096,128]{2,0,1:T(1,128)}), f32[1,4096,128]{2,0,1:T(1,128)}, u32[]{:S(2)}, u32[]{:S(2)}) %all-to-all-start.7) | async-done | bytes 2097184 | tf_op jit(solution)/shard_map/all_to_all | solution.py:163
  (266 shorter events, 205.6 us)
Async XLA Ops:
  41.6 15.2 %copy-start.10 = (bf16[1,128,512]{2,1,0:T(8,128)(2,1)S(1)}, bf16[1,128,512]{2,1,0:T(8,128)(2,1)}, u32[]{:S(2)}) copy-start(bf16[1,128,512]{2,1,0:T(8,128)(2,1)} %param.14) | copy-start | bytes 393220
  42.7 56.8 %all-to-all-start.3 = ((bf16[32,2,8192]{2,1,0:T(2,128)(2,1)}), bf16[32,2,8192]{2,1,0:T(2,128)(2,1)S(1)}, u32[]{:S(2)}, u32[]{:S(2)}) async-start(bf16[32,2,8192]{2,1,0:T(2,128)(2,1)} %reshape.435), calls=%async_computation.3 | async-start | bytes 2097152 | tf_op jit(solution)/shard_map/all_to_all | solution.py:121
  97.2 11.7 %copy-start.13 = (s32[1,128]{1,0:T(1,128)S(1)}, s32[1,128]{1,0:T(1,128)}, u32[]{:S(2)}) copy-start(s32[1,128]{1,0:T(1,128)} %param.19) | copy-start | bytes 1540
  97.2 127.1 %copy-start.8 = (bf16[1,128,4096]{2,1,0:T(8,128)(2,1)S(1)}, bf16[1,128,4096]{2,1,0:T(8,128)(2,1)}, u32[]{:S(2)}) copy-start(bf16[1,128,4096]{2,1,0:T(8,128)(2,1)} %param.16) | copy-start | bytes 3145732
  99.5 124.8 %copy-start.4 = (bf16[32,2,8192]{2,1,0:T(2,128)(2,1)}, bf16[32,2,8192]{2,1,0:T(2,128)(2,1)S(1)}, u32[]{:S(2)}) copy-start(bf16[32,2,8192]{2,1,0:T(2,128)(2,1)S(1)} %all-to-all-done.3) | copy-start | bytes 3145732
  99.5 151.4 %all-to-all-start.1 = ((bf16[32,2,8192]{2,1,0:T(2,128)(2,1)}), bf16[32,2,8192]{2,1,0:T(2,128)(2,1)}, u32[]{:S(2)}, u32[]{:S(2)}) async-start(bf16[32,2,8192]{2,1,0:T(2,128)(2,1)} %reshape.431), calls=%async_computation.1 | async-start | bytes 2097152 | tf_op jit(solution)/shard_map/all_to_all | solution.py:120
  250.9 7.9 copy-start.7
  250.9 36.4 %all-to-all-start.2 = ((bf16[32,2,8192]{2,1,0:T(2,128)(2,1)}), bf16[32,2,8192]{2,1,0:T(2,128)(2,1)}, u32[]{:S(2)}, u32[]{:S(2)}) async-start(bf16[32,2,8192]{2,1,0:T(2,128)(2,1)} %reshape.433), calls=%async_computation.2 | async-start | bytes 2097152 | tf_op jit(solution)/shard_map/all_to_all | solution.py:119
  284.9 11.8 %copy-start.12 = (s32[1,21]{1,0:T(1,128)S(1)}, s32[1,21]{1,0:T(1,128)}, u32[]{:S(2)}) copy-start(s32[1,21]{1,0:T(1,128)} %param.17) | copy-start | bytes 256
  284.9 12.3 %copy-start.14 = (s32[1,64]{1,0:T(1,128)S(1)}, s32[1,64]{1,0:T(1,128)}, u32[]{:S(2)}) copy-start(s32[1,64]{1,0:T(1,128)} %param.18) | copy-start | bytes 772
  285.0 14.5 %copy-start.5 = (bf16[32,2,8192]{2,1,0:T(2,128)(2,1)S(1)}, bf16[32,2,8192]{2,1,0:T(2,128)(2,1)}, u32[]{:S(2)}) copy-start(bf16[32,2,8192]{2,1,0:T(2,128)(2,1)} %copy-done.4) | copy-start | bytes 3145732
  287.2 34.1 %all-to-all-start = ((bf16[32,2,8192]{2,1,0:T(2,128)(2,1)}), bf16[32,2,8192]{2,1,0:T(2,128)(2,1)}, u32[]{:S(2)}, u32[]{:S(2)}) async-start(bf16[32,2,8192]{2,1,0:T(2,128)(2,1)} %reshape.429), calls=%async_computation | async-start | bytes 2097152 | tf_op jit(solution)/shard_map/all_to_all | solution.py:118
  306.5 1.2 copy-start.6
  326.9 5.3 copy-start.2
  326.9 5.3 copy-start.3
  572.4 2.2 copy-start.9
  572.5 3.1 copy-start.11
  618.3 48.9 %all-to-all-start.5 = ((bf16[32,2,8192]{2,1,0:T(2,128)(2,1)}), bf16[32,2,8192]{2,1,0:T(2,128)(2,1)}, u32[]{:S(2)}, u32[]{:S(2)}) async-start(bf16[32,2,8192]{2,1,0:T(2,128)(2,1)} %reshape.439), calls=%async_computation.5 | async-start | bytes 2097152 | tf_op jit(solution)/shard_map/all_to_all | solution.py:159
  666.0 10.3 %copy-start = (f32[4096,1,128]{2,0,1:T(8,128)S(1)}, f32[4096,1,128]{2,0,1:T(8,128)}, u32[]{:S(2)}) copy-start(f32[4096,1,128]{2,0,1:T(8,128)} %get-tuple-element.172) | copy-start | bytes 6291460
  667.2 33.6 %all-to-all-start.4 = ((bf16[32,2,8192]{2,1,0:T(2,128)(2,1)}), bf16[32,2,8192]{2,1,0:T(2,128)(2,1)S(1)}, u32[]{:S(2)}, u32[]{:S(2)}) async-start(bf16[32,2,8192]{2,1,0:T(2,128)(2,1)} %reshape.437), calls=%async_computation.4 | async-start | bytes 2097152 | tf_op jit(solution)/shard_map/all_to_all | solution.py:158
  756.0 57.7 %all-to-all-start.7 = ((f32[1,4096,128]{2,0,1:T(1,128)}), f32[1,4096,128]{2,0,1:T(1,128)}, u32[]{:S(2)}, u32[]{:S(2)}) async-start(f32[1,4096,128]{2,0,1:T(1,128)} %bitcast.54), calls=%async_computation.7 | async-start | bytes 4194304 | tf_op jit(solution)/shard_map/all_to_all | solution.py:163
  773.9 3.6 copy-start.1
where the time goes:
time: 827 us; the launch traced here: 817 us
  local copies, waits for them, and re-layouts  276 us (33%)
  blocking collectives  169 us (20%)
  other arithmetic  157 us (19%)
  matrix products  81.6 us (10%)
  starting transfers between devices  66.9 us (8%)
  waiting for transfers between devices  52.5 us (6%)
  loops' own time  11.1 us (1%)
    unnamed x6, other arithmetic  137 us
    psum x1, blocking collectives, shards(): target_total = lax.psum(local_count, ('dp', 'ctx'))  114 us
    all_to_all x1, blocking collectives, shards(): lax.all_to_all(dk_stored, 'ctx', split_axis=1, concat_axis=2, tiled=True)  55.2 us
    unnamed x54, local copies, waits for them, and re-layouts  42.2 us
    all_to_all x1, waiting for transfers between devices, shards(): lax.all_to_all(dv_stored, 'ctx', split_axis=1, concat_axis=2, tiled=True)  35.2 us
    dynamic_slice x16, local copies, waits for them, and re-layouts, step(): lax.dynamic_slice_in_dim(acc_keys, k_start, 2 * span, 0) + key_part  32.3 us
    dynamic_update_slice x24, local copies, waits for them, and re-layouts, band_pass(): lax.scan(step, (zeros_acc, zeros_acc), jnp.arange(pack_rows // span, dtyp...  27.2 us
    dynamic_slice x16, local copies, waits for them, and re-layouts, step(): lax.dynamic_slice_in_dim(acc_values, k_start, 2 * span, 0) + value_part  25.3 us
  transfers between devices with their start and end apart: 7, of which 3 were waited for; matrix products, arithmetic and copies ran while one was open for 23% of the time, Pallas kernels for 0%

commit v1 on v0

v1 whole, which is shorter than its diff:
```python
import math

import jax
import jax.numpy as jnp
from jax import lax
from jax.experimental import pallas as pl
from jax.experimental.pallas import tpu as pltpu
from jax.sharding import PartitionSpec as P

HEAD_WIDTH = 128
QUERY_HEADS = 32
KEY_VALUE_HEADS = 4
ALIGN_TOKENS = 64
MOST = 8
GROUP = QUERY_HEADS // KEY_VALUE_HEADS
SPAN = MOST * ALIGN_TOKENS
LOG2E = math.log2(math.e)
SCALE = 1.0 / math.sqrt(HEAD_WIDTH)
HIDDEN = -1e30
CHUNK_HEADS = 4


def dot_nt(a, b):
    return lax.dot_general(a, b, (((1,), (1,)), ((), ())), preferred_element_type=jnp.float32)


def dot_nn(a, b):
    return lax.dot_general(a, b, (((1,), (0,)), ((), ())), preferred_element_type=jnp.float32)


def attention_kernel(
    back_ref,
    q_ref,
    g_ref,
    own_ref,
    near_ref,
    mid_ref,
    far_ref,
    last_ref,
    out_ref,
    dq_ref,
    own_part,
    near_part,
    mid_part,
    far_part,
    last_part,
    acc_ref,
):
    width = HEAD_WIDTH
    block = ALIGN_TOKENS
    window = jnp.concatenate(
        [last_ref[...], far_ref[...], mid_ref[...], near_ref[...], own_ref[...]], axis=0
    )
    keys, values = window[:, :width], window[:, width:]
    keys_t, values_t = jnp.transpose(keys), jnp.transpose(values)
    cols = CHUNK_HEADS * block
    causal = lax.broadcasted_iota(jnp.int32, (block, cols), 0) <= (
        lax.broadcasted_iota(jnp.int32, (block, cols), 1) & (block - 1)
    )
    rows = window.shape[0]
    acc_ref[SPAN:rows, :] = jnp.zeros((rows - SPAN, 2 * width), jnp.float32)
    for t in range(rows // block - MOST + 1):
        lo = t * block
        back = back_ref[t]
        k_t, v_t = keys[lo : lo + SPAN], values[lo : lo + SPAN]
        kt_t, vt_t = keys_t[:, lo : lo + SPAN], values_t[:, lo : lo + SPAN]
        dk = dv = None
        for c in range(GROUP // CHUNK_HEADS):
            heads = range(c * CHUNK_HEADS, (c + 1) * CHUNK_HEADS)
            q = jnp.concatenate(
                [q_ref[lo : lo + block, h * width : (h + 1) * width] for h in heads], axis=0
            )
            g = jnp.concatenate(
                [g_ref[lo : lo + block, h * width : (h + 1) * width] for h in heads], axis=0
            )
            s = dot_nt(k_t, q)
            dp = dot_nt(v_t, g)
            parts = [
                s[b * block : (b + 1) * block] + jnp.where(b >= MOST - 1 - back, 0.0, HIDDEN)
                for b in range(MOST - 1)
            ]
            parts.append(jnp.where(causal, s[SPAN - block :], HIDDEN))
            s = jnp.concatenate(parts, axis=0)
            peak = jnp.max(s, axis=0, keepdims=True)
            e = jnp.exp2((s - peak) * (SCALE * LOG2E))
            p = e * (1.0 / jnp.sum(e, axis=0, keepdims=True))
            p_low = p.astype(jnp.bfloat16)
            delta = jnp.sum(p * dp, axis=0, keepdims=True)
            ds = (p * (dp - delta)).astype(jnp.bfloat16)
            dk_c, dv_c = dot_nn(ds, q), dot_nn(p_low, g)
            dk, dv = (dk_c, dv_c) if dk is None else (dk + dk_c, dv + dv_c)
            out_c = jnp.transpose(dot_nn(vt_t, p_low)).astype(jnp.bfloat16)
            dq_c = jnp.transpose(dot_nn(kt_t, ds) * SCALE).astype(jnp.bfloat16)
            for i, h in enumerate(heads):
                at = (slice(lo, lo + block), slice(h * width, (h + 1) * width))
                out_ref[at] = out_c[i * block : (i + 1) * block]
                dq_ref[at] = dq_c[i * block : (i + 1) * block]
        part = jnp.concatenate([dk * SCALE, dv], axis=1)
        if t == 0:
            acc_ref[0:SPAN, :] = part
        else:
            acc_ref[lo : lo + SPAN, :] = acc_ref[lo : lo + SPAN, :] + part
    at = 0
    for ref in (last_part, far_part, mid_part, near_part, own_part):
        ref[...] = acc_ref[at : at + ref.shape[0], :].astype(ref.dtype)
        at += ref.shape[0]


def attention(back, queries, grads, own, near, mid, far, last):
    tokens = queries.shape[0]
    tail = last.shape[0]
    columns = lambda n, w: pl.BlockSpec((n, w), lambda i, *_: (0, i))
    pair = 2 * HEAD_WIDTH
    wide = GROUP * HEAD_WIDTH
    kv_specs = [columns(tokens, pair)] * 4 + [columns(tail, pair)]
    shape = jax.ShapeDtypeStruct
    return pl.pallas_call(
        attention_kernel,
        grid_spec=pltpu.PrefetchScalarGridSpec(
            num_scalar_prefetch=1,
            grid=(KEY_VALUE_HEADS,),
            in_specs=[columns(tokens, wide)] * 2 + kv_specs,
            out_specs=[columns(tokens, wide)] * 2 + kv_specs,
            scratch_shapes=[pltpu.VMEM((4 * tokens + tail, pair), jnp.float32)],
        ),
        out_shape=[
            shape(queries.shape, jnp.bfloat16),
            shape(queries.shape, jnp.bfloat16),
            shape(own.shape, jnp.float32),
            shape(own.shape, jnp.bfloat16),
            shape(own.shape, jnp.bfloat16),
            shape(own.shape, jnp.bfloat16),
            shape(last.shape, jnp.bfloat16),
        ],
        compiler_params=pltpu.CompilerParams(vmem_limit_bytes=48 * 1024 * 1024),
        name="attention",
    )(back, queries, grads, own, near, mid, far, last)


def blocks_back(lengths, order, first, count):
    ends = jnp.sum(
        jnp.where(
            jnp.arange(lengths.shape[0])[:, None] >= jnp.arange(lengths.shape[0])[None, :],
            lengths[None, :],
            0,
        ),
        axis=1,
    )
    places = lax.dynamic_slice_in_dim(order, first, count, 0)
    starts = jnp.max(jnp.where(ends[None, :] <= places[:, None], ends[None, :], 0), axis=1)
    return places - starts


def count_ones(target_mask):
    local = jnp.sum(target_mask.astype(jnp.float32))
    total = local
    for axis in ("dp", "ctx"):
        n = lax.axis_size(axis)
        sent = jnp.broadcast_to(total, (n, 1, 128))
        total = jnp.sum(lax.all_to_all(sent, axis, split_axis=0, concat_axis=0)[:, 0, 0])
    return total


def shards(
    queries, key_head_states, value_head_states, out_grad, doc_blocks, block_order, target_mask
):
    tokens = queries.shape[1]
    ctx_count = lax.axis_size("ctx")
    pack_rows = tokens * ctx_count
    heads, width = KEY_VALUE_HEADS, HEAD_WIDTH

    def shift(array, steps):
        pairs = [
            (i, i + steps) for i in range(ctx_count) if 0 <= i + steps < ctx_count
        ]
        return lax.ppermute(array, "ctx", pairs)

    own = jnp.concatenate(
        [
            key_head_states.reshape(tokens, heads, 1, width),
            value_head_states.reshape(tokens, heads, 1, width),
        ],
        axis=2,
    ).reshape(tokens, 2 * heads * width)
    tail = SPAN - ALIGN_TOKENS - 3 * tokens
    far_to_near = [
        shift(own[tokens - tail :], 4),
        shift(own, 3),
        shift(own, 2),
        shift(own, 1),
    ]
    last, far, mid, near = far_to_near
    total = count_ones(target_mask)
    factor = lax.axis_size("dp") * pack_rows / total
    grads = out_grad[0] * target_mask[0].astype(jnp.bfloat16)[:, None]
    blocks = tokens // ALIGN_TOKENS
    back = blocks_back(
        doc_blocks[0], block_order[0], lax.axis_index("ctx") * blocks, blocks
    )
    attended, dq, own_part, near_part, mid_part, far_part, last_part = attention(
        back, queries[0], grads, own, near, mid, far, last
    )
    last_back = shift(last_part, -4)
    far_back = shift(far_part, -3)
    mid_back = shift(mid_part, -2)
    near_back = shift(near_part, -1)
    grad_queries = (dq.astype(jnp.float32) * factor).astype(jnp.bfloat16)
    whole = own_part
    for part in (near_back, mid_back, far_back):
        whole = whole + part.astype(jnp.float32)
    whole = whole + jnp.pad(last_back.astype(jnp.float32), ((tokens - tail, 0), (0, 0)))
    whole = (whole * factor).astype(jnp.bfloat16).reshape(tokens, heads, 2, width)
    grad_keys = whole[:, :, 0].reshape(1, tokens, heads * width)
    grad_values = whole[:, :, 1].reshape(1, tokens, heads * width)
    return (attended[None], grad_queries[None], grad_keys, grad_values)


def solution(mesh):
    placed = (
        P("dp", "ctx", None),
        P("dp", "ctx", None),
        P("dp", "ctx", None),
        P("dp", "ctx", None),
        P("dp", None),
        P("dp", None),
        P("dp", "ctx"),
    )
    return jax.shard_map(
        shards,
        mesh=mesh,
        in_specs=placed,
        out_specs=(
            P("dp", "ctx", None),
            P("dp", "ctx", None),
            P("dp", "ctx", None),
            P("dp", "ctx", None),
        ),
        check_vma=False,
    )
```

time: 827 us -> 123 us (0.15)
  the two profiles are of different devices: /device:TPU:1 before, /device:TPU:64 now
where the time goes in v1:
time: 123 us; the launch traced here: 122 us
  waiting for transfers between devices  49.2 us (40%)
  starting transfers between devices  44.1 us (36%)
  Pallas kernels  13.8 us (11%)
  local copies, waits for them, and re-layouts  7.86 us (6%)
  other arithmetic  5.93 us (5%)
  between operations  1.57 us (1%)
    ppermute x8, waiting for transfers between devices, shift(): return lax.ppermute(array, 'ctx', pairs)  35.1 us
    ppermute x8, starting transfers between devices, shift(): return lax.ppermute(array, 'ctx', pairs)  26.4 us
    all_to_all x2, starting transfers between devices, count_ones(): lax.all_to_all(sent, axis, split_axis=0, concat_axis=0)[:, 0, 0]  17.7 us
    all_to_all x2, waiting for transfers between devices, count_ones(): lax.all_to_all(sent, axis, split_axis=0, concat_axis=0)[:, 0, 0]  14.1 us
    pallas_call x1, Pallas kernels, attention(): pl.pallas_call(attention_kernel, grid_spec=pltpu.PrefetchScalarGridSpec(n...  13.8 us
    broadcast_in_dim x2, local copies, waits for them, and re-layouts, count_ones(): sent = jnp.broadcast_to(total, (n, 1, 128))  2.51 us
  transfers between devices with their start and end apart: 10, of which 4 were waited for; matrix products, arithmetic and copies ran while one was open for 6% of the time, Pallas kernels for 0%

profile of v1, /device:TPU:64, one launch (start us, length us, event | category | flops | bytes accessed | tf_op | source)
XLA Modules:
  0.0 122.4 jit_solution(14042016069217551882)
XLA Ops:
  0.6 1.3 %reshape.35 = bf16[128,4,1,128]{3,2,1,0:T(2,128)(2,1)S(1)} reshape(bf16[1,128,512]{2,1,0:T(8,128)(2,1)} %param.8) | data formatting | bytes 262144 | tf_op jit(solution)/shard_map/reshape | solution.py:180
  1.9 1.3 %reshape.36 = bf16[128,4,1,128]{3,2,1,0:T(2,128)(2,1)S(1)} reshape(bf16[1,128,512]{2,1,0:T(8,128)(2,1)} %param.9) | data formatting | bytes 262144 | tf_op jit(solution)/shard_map/reshape | solution.py:181
  3.3 0.0 copy-start.2
  3.3 0.0 copy-start.3
  3.3 0.0 copy-start.1
  3.3 0.6 pad_maximum_fusion
  3.9 0.2 reshape.33.own_ref
  4.1 4.3 %collective-permute-start = (bf16[128,1024]{1,0:T(8,128)(2,1)S(1)}, bf16[128,1024]{1,0:T(8,128)(2,1)S(1)}, u32[]{:S(2)}, u32[]{:S(2)}) collective-permute-start(bf16[128,1024]{1,0:T(8,128)(2,1)S(1)} %reshape.33.own_ref), channel_id=1, source_target_pairs={{0,1},{1,2},{2,3},{3,4},{4,5},{5,6},{6,7},{7,8},{8,9},{9,10},{10,1... | collective-permute-start | bytes 786440 | tf_op jit(solution)/shard_map/ppermute | solution.py:176
  8.4 7.3 %collective-permute-start.1 = (bf16[128,1024]{1,0:T(8,128)(2,1)S(1)}, bf16[128,1024]{1,0:T(8,128)(2,1)S(1)}, u32[]{:S(2)}, u32[]{:S(2)}) collective-permute-start(bf16[128,1024]{1,0:T(8,128)(2,1)S(1)} %reshape.33.own_ref), channel_id=1, source_target_pairs={{0,2},{1,3},{2,4},{3,5},{4,6},{5,7},{6,8},{7,9},{8,10},{9,11},{10,... | collective-permute-start | bytes 786440 | tf_op jit(solution)/shard_map/ppermute | solution.py:176
  15.7 5.2 %collective-permute-start.2 = (bf16[128,1024]{1,0:T(8,128)(2,1)S(1)}, bf16[128,1024]{1,0:T(8,128)(2,1)S(1)}, u32[]{:S(2)}, u32[]{:S(2)}) collective-permute-start(bf16[128,1024]{1,0:T(8,128)(2,1)S(1)} %reshape.33.own_ref), channel_id=1, source_target_pairs={{0,3},{1,4},{2,5},{3,6},{4,7},{5,8},{6,9},{7,10},{8,11},{9,12},{10... | collective-permute-start | bytes 786440 | tf_op jit(solution)/shard_map/ppermute | solution.py:176
  20.9 0.3 fusion.1
  21.2 0.1 slice.19
  21.3 2.4 %collective-permute-start.3 = (bf16[64,1024]{1,0:T(8,128)(2,1)S(1)}, bf16[64,1024]{1,0:T(8,128)(2,1)S(1)}, u32[]{:S(2)}, u32[]{:S(2)}) collective-permute-start(bf16[64,1024]{1,0:T(8,128)(2,1)S(1)} %slice.19), channel_id=1, source_target_pairs={{0,4},{1,5},{2,6},{3,7},{4,8},{5,9},{6,10},{7,11},{8,12},{9,13},{1... | collective-permute-start | bytes 393224 | tf_op jit(solution)/shard_map/ppermute | solution.py:176
  23.7 0.0 copy-done.2
  23.7 0.6 convert_reduce_fusion
  24.4 1.2 %broadcast_in_dim.47 = f32[16,1,128]{2,1,0:T(1,128)} broadcast(f32[]{:T(128)} %convert_reduce_fusion), dimensions={} | broadcast | bytes 8196 | tf_op jit(solution)/shard_map/broadcast_in_dim | solution.py:159
  25.6 7.2 %all-to-all-start = ((f32[16,1,128]{2,1,0:T(1,128)}), f32[16,1,128]{2,1,0:T(1,128)S(1)}, u32[]{:S(2)}, u32[]{:S(2)}) async-start(f32[16,1,128]{2,1,0:T(1,128)} %broadcast_in_dim.47), calls=%async_computation | async-start | bytes 16384 | tf_op jit(solution)/shard_map/all_to_all | solution.py:160
  32.8 0.0 copy-done.3
  32.8 0.1 select_reduce_fusion
  33.0 0.0 copy-done.1
  33.0 0.1 dynamic-slice_bitcast_fusion
  33.0 0.0 copy-start
  33.0 1.4 %bitcast_multiply_fusion.g_ref = bf16[128,4096]{1,0:T(8,128)(2,1)S(1)} fusion(bf16[1,128,4096]{2,1,0:T(8,128)(2,1)} %param.10, bf16[128]{0:T(256)(128)(2,1)S(1)} %convert_bitcast_fusion), kind=kLoop, calls=%fused_computation.2 | loop fusion | flops 524288 | bytes 2097408 | tf_op jit(solution)/shard_map/mul | solution.py:195
  34.5 0.2 fusion.2
  34.7 5.6 %all-to-all-done = f32[16,1,128]{2,1,0:T(1,128)S(1)} async-done(((f32[16,1,128]{2,1,0:T(1,128)}), f32[16,1,128]{2,1,0:T(1,128)S(1)}, u32[]{:S(2)}, u32[]{:S(2)}) %all-to-all-start) | async-done | bytes 8224 | tf_op jit(solution)/shard_map/all_to_all | solution.py:160
  40.3 0.6 slice_reduce_fusion.1
  40.9 1.3 %broadcast_in_dim.48 = f32[32,1,128]{2,1,0:T(1,128)} broadcast(f32[]{:T(128)} %slice_reduce_fusion.1), dimensions={} | broadcast | bytes 16388 | tf_op jit(solution)/shard_map/broadcast_in_dim | solution.py:159
  42.2 10.5 %all-to-all-start.1 = ((f32[32,1,128]{2,1,0:T(1,128)}), f32[32,1,128]{2,1,0:T(1,128)S(1)}, u32[]{:S(2)}, u32[]{:S(2)}) async-start(f32[32,1,128]{2,1,0:T(1,128)} %broadcast_in_dim.48), calls=%async_computation.1 | async-start | bytes 32768 | tf_op jit(solution)/shard_map/all_to_all | solution.py:160
  52.7 0.1 fusion.4.back_ref
  52.7 8.5 %all-to-all-done.1 = f32[32,1,128]{2,1,0:T(1,128)S(1)} async-done(((f32[32,1,128]{2,1,0:T(1,128)}), f32[32,1,128]{2,1,0:T(1,128)S(1)}, u32[]{:S(2)}, u32[]{:S(2)}) %all-to-all-start.1) | async-done | bytes 16416 | tf_op jit(solution)/shard_map/all_to_all | solution.py:160
  61.2 0.6 slice_reduce_fusion
  62.5 0.0 collective-permute-done.3.last_ref
  62.5 0.0 collective-permute-done.near_ref
  62.5 0.0 collective-permute-done.1.mid_ref
  62.6 0.0 collective-permute-done.2.far_ref
  62.6 0.0 copy-done
  62.6 13.8 %attention.1 = (bf16[128,4096]{1,0:T(8,128)(2,1)}, bf16[128,4096]{1,0:T(8,128)(2,1)S(1)}, f32[128,1024]{1,0:T(8,128)S(1)}, bf16[128,1024]{1,0:T(8,128)(2,1)S(1)}...) custom-call(s32[2]{0:T(128)S(1)} %fusion.4.back_ref, ...), custom_call_target="tpu_custom_call" | custom-call | tf_op jit(solution)/shard_map/attention/pallas_call | solution.py:117
  76.3 3.3 %collective-permute-start.4 = (bf16[128,1024]{1,0:T(8,128)(2,1)S(1)}, bf16[128,1024]{1,0:T(8,128)(2,1)S(1)}, u32[]{:S(2)}, u32[]{:S(2)}) collective-permute-start(bf16[128,1024]{1,0:T(8,128)(2,1)S(1)} %get-tuple-element.14), channel_id=1, source_target_pairs={{1,0},{2,1},{3,2},{4,3},{5,4},{6,5},{7,6},{8,7},{9,8},{10,9},{11,1... | collective-permute-start | bytes 786440 | tf_op jit(solution)/shard_map/ppermute | solution.py:176
  79.6 1.3 %collective-permute-start.5 = (bf16[128,1024]{1,0:T(8,128)(2,1)S(1)}, bf16[128,1024]{1,0:T(8,128)(2,1)S(1)}, u32[]{:S(2)}, u32[]{:S(2)}) collective-permute-start(bf16[128,1024]{1,0:T(8,128)(2,1)S(1)} %get-tuple-element.15), channel_id=1, source_target_pairs={{2,0},{3,1},{4,2},{5,3},{6,4},{7,5},{8,6},{9,7},{10,8},{11,9},{12,... | collective-permute-start | bytes 786440 | tf_op jit(solution)/shard_map/ppermute | solution.py:176
  80.9 1.3 %collective-permute-start.6 = (bf16[128,1024]{1,0:T(8,128)(2,1)S(1)}, bf16[128,1024]{1,0:T(8,128)(2,1)S(1)}, u32[]{:S(2)}, u32[]{:S(2)}) collective-permute-start(bf16[128,1024]{1,0:T(8,128)(2,1)S(1)} %get-tuple-element.16), channel_id=1, source_target_pairs={{3,0},{4,1},{5,2},{6,3},{7,4},{8,5},{9,6},{10,7},{11,8},{12,9},{13... | collective-permute-start | bytes 786440 | tf_op jit(solution)/shard_map/ppermute | solution.py:176
  82.2 1.3 %collective-permute-start.7 = (bf16[64,1024]{1,0:T(8,128)(2,1)S(1)}, bf16[64,1024]{1,0:T(8,128)(2,1)S(1)}, u32[]{:S(2)}, u32[]{:S(2)}) collective-permute-start(bf16[64,1024]{1,0:T(8,128)(2,1)S(1)} %get-tuple-element.17), channel_id=1, source_target_pairs={{4,0},{5,1},{6,2},{7,3},{8,4},{9,5},{10,6},{11,7},{12,8},{13,9},{1... | collective-permute-start | bytes 393224 | tf_op jit(solution)/shard_map/ppermute | solution.py:176
  83.5 1.2 fusion
  84.7 34.4 %collective-permute-done.7 = bf16[64,1024]{1,0:T(8,128)(2,1)S(1)} collective-permute-done((bf16[64,1024]{1,0:T(8,128)(2,1)S(1)}, bf16[64,1024]{1,0:T(8,128)(2,1)S(1)}, u32[]{:S(2)}, u32[]{:S(2)}) %collective-permute-start.7) | collective-permute-done | bytes 131104 | tf_op jit(solution)/shard_map/ppermute | solution.py:176
  119.1 0.0 collective-permute-done.4
  119.1 0.0 collective-permute-done.5
  119.1 0.7 collective-permute-done.6
  119.8 0.2 multiply_convert_fusion.1
  120.0 0.2 reshape.34
  120.2 0.4 fusion.3
  120.5 0.2 copy.35
  120.7 0.8 copy.31
  121.5 0.2 copy.36
  121.6 0.8 copy.32
  (1 shorter events, 0.0 us)
Async XLA Ops:
  3.3 20.5 %copy-start.2 = (s32[1,128]{1,0:T(1,128)S(1)}, s32[1,128]{1,0:T(1,128)}, u32[]{:S(2)}) copy-start(s32[1,128]{1,0:T(1,128)} %param.13) | copy-start | bytes 1540
  3.3 29.6 %copy-start.3 = (s32[1,21]{1,0:T(1,128)S(1)}, s32[1,21]{1,0:T(1,128)}, u32[]{:S(2)}) copy-start(s32[1,21]{1,0:T(1,128)} %param.11) | copy-start | bytes 256
  3.3 29.7 %copy-start.1 = (s32[1,64]{1,0:T(1,128)S(1)}, s32[1,64]{1,0:T(1,128)}, u32[]{:S(2)}) copy-start(s32[1,64]{1,0:T(1,128)} %param.12) | copy-start | bytes 772
  4.1 58.5 %collective-permute-start = (bf16[128,1024]{1,0:T(8,128)(2,1)S(1)}, bf16[128,1024]{1,0:T(8,128)(2,1)S(1)}, u32[]{:S(2)}, u32[]{:S(2)}) collective-permute-start(bf16[128,1024]{1,0:T(8,128)(2,1)S(1)} %reshape.33.own_ref), channel_id=1, source_target_pairs={{0,1},{1,2},{2,3},{3,4},{4,5},{5,6},{6,7},{7,8},{8,9},{9,10},{10,1... | collective-permute-start | bytes 786440 | tf_op jit(solution)/shard_map/ppermute | solution.py:176
  8.4 54.2 %collective-permute-start.1 = (bf16[128,1024]{1,0:T(8,128)(2,1)S(1)}, bf16[128,1024]{1,0:T(8,128)(2,1)S(1)}, u32[]{:S(2)}, u32[]{:S(2)}) collective-permute-start(bf16[128,1024]{1,0:T(8,128)(2,1)S(1)} %reshape.33.own_ref), channel_id=1, source_target_pairs={{0,2},{1,3},{2,4},{3,5},{4,6},{5,7},{6,8},{7,9},{8,10},{9,11},{10,... | collective-permute-start | bytes 786440 | tf_op jit(solution)/shard_map/ppermute | solution.py:176
  15.7 46.9 %collective-permute-start.2 = (bf16[128,1024]{1,0:T(8,128)(2,1)S(1)}, bf16[128,1024]{1,0:T(8,128)(2,1)S(1)}, u32[]{:S(2)}, u32[]{:S(2)}) collective-permute-start(bf16[128,1024]{1,0:T(8,128)(2,1)S(1)} %reshape.33.own_ref), channel_id=1, source_target_pairs={{0,3},{1,4},{2,5},{3,6},{4,7},{5,8},{6,9},{7,10},{8,11},{9,12},{10... | collective-permute-start | bytes 786440 | tf_op jit(solution)/shard_map/ppermute | solution.py:176
  21.3 41.2 %collective-permute-start.3 = (bf16[64,1024]{1,0:T(8,128)(2,1)S(1)}, bf16[64,1024]{1,0:T(8,128)(2,1)S(1)}, u32[]{:S(2)}, u32[]{:S(2)}) collective-permute-start(bf16[64,1024]{1,0:T(8,128)(2,1)S(1)} %slice.19), channel_id=1, source_target_pairs={{0,4},{1,5},{2,6},{3,7},{4,8},{5,9},{6,10},{7,11},{8,12},{9,13},{1... | collective-permute-start | bytes 393224 | tf_op jit(solution)/shard_map/ppermute | solution.py:176
  25.6 14.7 %all-to-all-start = ((f32[16,1,128]{2,1,0:T(1,128)}), f32[16,1,128]{2,1,0:T(1,128)S(1)}, u32[]{:S(2)}, u32[]{:S(2)}) async-start(f32[16,1,128]{2,1,0:T(1,128)} %broadcast_in_dim.47), calls=%async_computation | async-start | bytes 16384 | tf_op jit(solution)/shard_map/all_to_all | solution.py:160
  33.0 29.5 %copy-start = (bf16[1,128,4096]{2,1,0:T(8,128)(2,1)S(1)}, bf16[1,128,4096]{2,1,0:T(8,128)(2,1)}, u32[]{:S(2)}) copy-start(bf16[1,128,4096]{2,1,0:T(8,128)(2,1)} %param.7) | copy-start | bytes 3145732
  42.2 19.0 %all-to-all-start.1 = ((f32[32,1,128]{2,1,0:T(1,128)}), f32[32,1,128]{2,1,0:T(1,128)S(1)}, u32[]{:S(2)}, u32[]{:S(2)}) async-start(f32[32,1,128]{2,1,0:T(1,128)} %broadcast_in_dim.48), calls=%async_computation.1 | async-start | bytes 32768 | tf_op jit(solution)/shard_map/all_to_all | solution.py:160
  76.3 42.8 %collective-permute-start.4 = (bf16[128,1024]{1,0:T(8,128)(2,1)S(1)}, bf16[128,1024]{1,0:T(8,128)(2,1)S(1)}, u32[]{:S(2)}, u32[]{:S(2)}) collective-permute-start(bf16[128,1024]{1,0:T(8,128)(2,1)S(1)} %get-tuple-element.14), channel_id=1, source_target_pairs={{1,0},{2,1},{3,2},{4,3},{5,4},{6,5},{7,6},{8,7},{9,8},{10,9},{11,1... | collective-permute-start | bytes 786440 | tf_op jit(solution)/shard_map/ppermute | solution.py:176
  79.6 39.5 %collective-permute-start.5 = (bf16[128,1024]{1,0:T(8,128)(2,1)S(1)}, bf16[128,1024]{1,0:T(8,128)(2,1)S(1)}, u32[]{:S(2)}, u32[]{:S(2)}) collective-permute-start(bf16[128,1024]{1,0:T(8,128)(2,1)S(1)} %get-tuple-element.15), channel_id=1, source_target_pairs={{2,0},{3,1},{4,2},{5,3},{6,4},{7,5},{8,6},{9,7},{10,8},{11,9},{12,... | collective-permute-start | bytes 786440 | tf_op jit(solution)/shard_map/ppermute | solution.py:176
  80.9 38.9 %collective-permute-start.6 = (bf16[128,1024]{1,0:T(8,128)(2,1)S(1)}, bf16[128,1024]{1,0:T(8,128)(2,1)S(1)}, u32[]{:S(2)}, u32[]{:S(2)}) collective-permute-start(bf16[128,1024]{1,0:T(8,128)(2,1)S(1)} %get-tuple-element.16), channel_id=1, source_target_pairs={{3,0},{4,1},{5,2},{6,3},{7,4},{8,5},{9,6},{10,7},{11,8},{12,9},{13... | collective-permute-start | bytes 786440 | tf_op jit(solution)/shard_map/ppermute | solution.py:176
  82.2 36.8 %collective-permute-start.7 = (bf16[64,1024]{1,0:T(8,128)(2,1)S(1)}, bf16[64,1024]{1,0:T(8,128)(2,1)S(1)}, u32[]{:S(2)}, u32[]{:S(2)}) collective-permute-start(bf16[64,1024]{1,0:T(8,128)(2,1)S(1)} %get-tuple-element.17), channel_id=1, source_target_pairs={{4,0},{5,1},{6,2},{7,3},{8,4},{9,5},{10,6},{11,7},{12,8},{13,9},{1... | collective-permute-start | bytes 393224 | tf_op jit(solution)/shard_map/ppermute | solution.py:176

commit v2 on v1

v2 whole, which is shorter than its diff:
```python
import math

import jax
import jax.numpy as jnp
from jax import lax
from jax.experimental import pallas as pl
from jax.experimental.pallas import tpu as pltpu
from jax.sharding import PartitionSpec as P

HEAD_WIDTH = 128
QUERY_HEADS = 32
KEY_VALUE_HEADS = 4
ALIGN_TOKENS = 64
MOST = 8
GROUP = QUERY_HEADS // KEY_VALUE_HEADS
SPAN = MOST * ALIGN_TOKENS
LOG2E = math.log2(math.e)
SCALE = 1.0 / math.sqrt(HEAD_WIDTH)
HIDDEN = -1e30


def dot_nt(a, b):
    return lax.dot_general(a, b, (((1,), (1,)), ((), ())), preferred_element_type=jnp.float32)


def dot_nn(a, b):
    return lax.dot_general(a, b, (((1,), (0,)), ((), ())), preferred_element_type=jnp.float32)


def dot_tn(a, b):
    return lax.dot_general(a, b, (((0,), (0,)), ((), ())), preferred_element_type=jnp.float32)


def fold_rows(x, op):
    folded = x[:8]
    for i in range(8, x.shape[0], 8):
        folded = op(folded, x[i : i + 8])
    return folded


def attention_kernel(
    back_ref,
    q_ref,
    g_ref,
    own_ref,
    near_ref,
    mid_ref,
    far_ref,
    fourth_ref,
    out_ref,
    dq_ref,
    own_part,
    near_part,
    mid_part,
    far_part,
    fourth_part,
    keys_acc,
    values_acc,
):
    width, block = HEAD_WIDTH, ALIGN_TOKENS
    shards_in = (fourth_ref, far_ref, mid_ref, near_ref, own_ref)
    keys = jnp.concatenate([ref[0] for ref in shards_in], axis=0)
    values = jnp.concatenate([ref[1] for ref in shards_in], axis=0)
    rows, tokens = keys.shape[0], own_ref.shape[1]
    count, cols = tokens // block, GROUP * block
    causal = lax.broadcasted_iota(jnp.int32, (block, cols), 0) <= (
        lax.broadcasted_iota(jnp.int32, (block, cols), 1) & (block - 1)
    )

    def heads_stacked(ref, t):
        return jnp.concatenate(
            [
                ref[t * block : (t + 1) * block, h * width : (h + 1) * width]
                for h in range(GROUP)
            ],
            axis=0,
        )

    def window(t):
        lo = rows - SPAN - (count - 1 - t) * block
        return slice(lo, lo + SPAN)

    def probabilities(t, s, dp):
        hidden = [jnp.where(b >= MOST - 1 - back_ref[t], 0.0, HIDDEN) for b in range(MOST - 1)]
        hidden.append(0.0)
        s = [s[b * block : (b + 1) * block] for b in range(MOST)]
        s[-1] = jnp.where(causal, s[-1], HIDDEN)
        dp = [dp[b * block : (b + 1) * block] for b in range(MOST)]
        peak = None
        for b in range(MOST):
            part = fold_rows(s[b], jnp.maximum) + hidden[b]
            peak = part if peak is None else jnp.maximum(peak, part)
        peak = jnp.max(peak, axis=0, keepdims=True)
        e, total, weighed = [], None, None
        for b in range(MOST):
            e.append(jnp.exp2((s[b] - (peak - hidden[b])) * (SCALE * LOG2E)))
            part, part_weighed = fold_rows(e[b], jnp.add), fold_rows(e[b] * dp[b], jnp.add)
            total = part if total is None else total + part
            weighed = part_weighed if weighed is None else weighed + part_weighed
        inverse = 1.0 / jnp.sum(total, axis=0, keepdims=True)
        delta = jnp.sum(weighed, axis=0, keepdims=True) * inverse
        p_low, ds = [], []
        for b in range(MOST):
            p = e[b] * inverse
            p_low.append(p.astype(jnp.bfloat16))
            ds.append((p * (dp[b] - delta)).astype(jnp.bfloat16))
        return jnp.concatenate(p_low, axis=0), jnp.concatenate(ds, axis=0)

    keys_acc[...] = jnp.zeros_like(keys_acc)
    values_acc[...] = jnp.zeros_like(values_acc)
    products = [
        (
            dot_nt(keys[window(t)], heads_stacked(q_ref, t)),
            dot_nt(values[window(t)], heads_stacked(g_ref, t)),
        )
        for t in range(count)
    ]
    for t in range(count):
        p_low, ds = probabilities(t, *products[t])
        keys_acc[window(t), :] += dot_nn(ds, heads_stacked(q_ref, t))
        values_acc[window(t), :] += dot_nn(p_low, heads_stacked(g_ref, t))
        out = dot_tn(p_low, values[window(t)]).astype(jnp.bfloat16)
        dq = (dot_tn(ds, keys[window(t)]) * SCALE).astype(jnp.bfloat16)
        for h in range(GROUP):
            place = (slice(t * block, (t + 1) * block), slice(h * width, (h + 1) * width))
            out_ref[place] = out[h * block : (h + 1) * block]
            dq_ref[place] = dq[h * block : (h + 1) * block]
    for i, ref in enumerate((fourth_part, far_part, mid_part, near_part, own_part)):
        part = slice(i * tokens, (i + 1) * tokens)
        ref[0] = (keys_acc[part, :] * SCALE).astype(ref.dtype)
        ref[1] = values_acc[part, :].astype(ref.dtype)


def in_hbm(array):
    return pltpu.with_memory_space_constraint(array, pltpu.HBM)


def attention(back, queries, grads, own, near, mid, far, fourth):
    tokens = queries.shape[0]
    wide = pl.BlockSpec((tokens, GROUP * HEAD_WIDTH), lambda i, *_: (0, i))
    pair = pl.BlockSpec((2, tokens, HEAD_WIDTH), lambda i, *_: (0, 0, i))
    shape = jax.ShapeDtypeStruct
    return pl.pallas_call(
        attention_kernel,
        grid_spec=pltpu.PrefetchScalarGridSpec(
            num_scalar_prefetch=1,
            grid=(KEY_VALUE_HEADS,),
            in_specs=[wide] * 2 + [pair] * 5,
            out_specs=[wide] * 2 + [pair] * 5,
            scratch_shapes=[pltpu.VMEM((5 * tokens, HEAD_WIDTH), jnp.float32)] * 2,
        ),
        out_shape=[shape(queries.shape, jnp.bfloat16)] * 2
        + [pltpu.HBM(own.shape, jnp.float32)]
        + [shape(own.shape, jnp.bfloat16)] * 4,
        compiler_params=pltpu.CompilerParams(vmem_limit_bytes=48 * 1024 * 1024),
        name="attention",
    )(back, queries, grads, own, *(in_hbm(x) for x in (near, mid, far, fourth)))


def blocks_back(lengths, order, first, count):
    ends = jnp.sum(
        jnp.where(
            jnp.arange(lengths.shape[0])[:, None] >= jnp.arange(lengths.shape[0])[None, :],
            lengths[None, :],
            0,
        ),
        axis=1,
    )
    places = lax.dynamic_slice_in_dim(order, first, count, 0)
    starts = jnp.max(jnp.where(ends[None, :] <= places[:, None], ends[None, :], 0), axis=1)
    return places - starts


def axis_total(value, axis):
    n = lax.axis_size(axis)
    sent = jnp.broadcast_to(value, (n, 1, HEAD_WIDTH))
    return jnp.sum(lax.all_to_all(sent, axis, split_axis=0, concat_axis=0)[:, 0, 0])


def after(value, *others):
    return lax.optimization_barrier((value, *others))[0]


def shards(
    queries, key_head_states, value_head_states, out_grad, doc_blocks, block_order, target_mask
):
    tokens = queries.shape[1]
    ctx_count = lax.axis_size("ctx")
    pack_rows = tokens * ctx_count

    def shift(array, steps):
        pairs = [(i, (i + steps) % ctx_count) for i in range(ctx_count)]
        return lax.ppermute(array, "ctx", pairs)

    own = jnp.concatenate([key_head_states, value_head_states], axis=0)
    fourth = shift(own, 4)
    near = shift(own, 1)
    pack_total = axis_total(jnp.sum(target_mask.astype(jnp.float32)), "ctx")
    mid = shift(near, 1)
    far = shift(fourth, -1)
    grads = out_grad[0] * target_mask[0].astype(jnp.bfloat16)[:, None]
    blocks = tokens // ALIGN_TOKENS
    back = blocks_back(doc_blocks[0], block_order[0], lax.axis_index("ctx") * blocks, blocks)
    back = after(back, pack_total)
    attended, dq, own_part, near_part, mid_part, far_part, fourth_part = attention(
        back, queries[0], grads, own, near, mid, far, fourth
    )
    mid_back = shift(mid_part, -1)
    far_on = shift(far_part, 1)
    near_sum = near_part + mid_back
    fourth_sum = fourth_part + far_on
    fourth_back = shift(fourth_sum, -4)
    near_back = shift(near_sum, -1)
    whole = own_part + near_back.astype(jnp.float32) + fourth_back.astype(jnp.float32)
    total = axis_total(after(pack_total, near_sum, fourth_sum), "dp")
    factor = lax.axis_size("dp") * pack_rows / after(total, whole)
    grad_queries = (dq.astype(jnp.float32) * factor).astype(jnp.bfloat16)
    whole = (whole * factor).astype(jnp.bfloat16)
    return (attended[None], grad_queries[None], whole[:1], whole[1:])


def solution(mesh):
    placed = (
        P("dp", "ctx", None),
        P("dp", "ctx", None),
        P("dp", "ctx", None),
        P("dp", "ctx", None),
        P("dp", None),
        P("dp", None),
        P("dp", "ctx"),
    )
    return jax.shard_map(
        shards,
        mesh=mesh,
        in_specs=placed,
        out_specs=(
            P("dp", "ctx", None),
            P("dp", "ctx", None),
            P("dp", "ctx", None),
            P("dp", "ctx", None),
        ),
        check_vma=False,
    )
```

time: 123 us -> 97.2 us (0.79)
  the two profiles are of different devices: /device:TPU:64 before, /device:TPU:1 now
where the time goes in v2:
time: 97.2 us; the launch traced here: 96.6 us
  starting transfers between devices  45.1 us (46%)
  blocking collectives  16.6 us (17%)
  Pallas kernels  11.5 us (12%)
  waiting for transfers between devices  10.1 us (10%)
  other arithmetic  6.46 us (7%)
  local copies, waits for them, and re-layouts  5.25 us (5%)
  between operations  1.52 us (2%)
    ppermute x8, starting transfers between devices, shift(): return lax.ppermute(array, 'ctx', pairs)  38.9 us
    all_to_all x1, blocking collectives, axis_total(): lax.all_to_all(sent, axis, split_axis=0, concat_axis=0)[:, 0, 0]  16.6 us
    pallas_call x1, Pallas kernels, attention(): pl.pallas_call(attention_kernel, grid_spec=pltpu.PrefetchScalarGridSpec(n...  11.5 us
    ppermute x8, waiting for transfers between devices, shift(): return lax.ppermute(array, 'ctx', pairs)  10.1 us
    all_to_all x1, starting transfers between devices, axis_total(): lax.all_to_all(sent, axis, split_axis=0, concat_axis=0)[:, 0, 0]  6.24 us
  transfers between devices with their start and end apart: 9, of which 3 were waited for; matrix products, arithmetic and copies ran while one was open for 7% of the time, Pallas kernels for 0%

profile of v2, /device:TPU:1, one launch (start us, length us, event | category | flops | bytes accessed | tf_op | source)
XLA Modules:
  0.0 96.6 jit_solution(18334726881857788223)
XLA Ops:
  0.6 0.9 constant_dynamic-update-slice_fusion.1
  1.5 0.9 constant_dynamic-update-slice_fusion.own_ref
  2.5 11.5 %collective-permute-start.2 = (bf16[2,128,512]{2,1,0:T(8,128)(2,1)S(1)}, bf16[2,128,512]{2,1,0:T(8,128)(2,1)S(1)}, u32[]{:S(2)}, u32[]{:S(2)}) collective-permute-start(bf16[2,128,512]{2,1,0:T(8,128)(2,1)S(1)} %constant_dynamic-update-slice_fusion.own_ref), channel_id=1, source_target_pairs={{0,4},{1,5},{2,6},{3,7},{4,8},{5,9},{6,10},{7,11},{8,12},{9,13},{1... | collective-permute-start | bytes 786440 | tf_op jit(solution)/shard_map/ppermute | solution.py:193
  13.9 3.1 %collective-permute-start = (bf16[2,128,512]{2,1,0:T(8,128)(2,1)S(1)}, bf16[2,128,512]{2,1,0:T(8,128)(2,1)S(1)}, u32[]{:S(2)}, u32[]{:S(2)}) collective-permute-start(bf16[2,128,512]{2,1,0:T(8,128)(2,1)S(1)} %constant_dynamic-update-slice_fusion.own_ref), channel_id=1, source_target_pairs={{0,1},{1,2},{2,3},{3,4},{4,5},{5,6},{6,7},{7,8},{8,9},{9,10},{10,1... | collective-permute-start | bytes 786440 | tf_op jit(solution)/shard_map/ppermute | solution.py:193
  17.0 1.3 %convert_reduce_fusion = f32[]{:T(128)} fusion(s32[1,128]{1,0:T(1,128)} %param.13), kind=kLoop, calls=%fused_computation.14 | loop fusion | flops 255 | bytes 516 | tf_op jit(solution)/shard_map/reduce_sum | solution.py:198
  18.3 1.3 %broadcast_in_dim.46 = f32[32,1,128]{2,1,0:T(1,128)} broadcast(f32[]{:T(128)} %convert_reduce_fusion), dimensions={} | broadcast | bytes 16388 | tf_op jit(solution)/shard_map/broadcast_in_dim | solution.py:176
  19.6 6.2 %all-to-all-start = ((f32[32,1,128]{2,1,0:T(1,128)}), f32[32,1,128]{2,1,0:T(1,128)S(1)}, u32[]{:S(2)}, u32[]{:S(2)}) async-start(f32[32,1,128]{2,1,0:T(1,128)} %broadcast_in_dim.46), calls=%async_computation | async-start | bytes 32768 | tf_op jit(solution)/shard_map/all_to_all | solution.py:177
  25.8 0.7 convert_bitcast_fusion
  26.5 0.0 copy-start.6
  26.5 0.0 copy-start.7
  26.5 0.0 copy-start
  26.5 1.4 %bitcast_multiply_fusion.g_ref = bf16[128,4096]{1,0:T(8,128)(2,1)S(1)} fusion(bf16[1,128,4096]{2,1,0:T(8,128)(2,1)} %param.10, bf16[128]{0:T(256)(128)(2,1)S(1)} %convert_bitcast_fusion), kind=kLoop, calls=%fused_computation.2 | loop fusion | flops 524288 | bytes 2097408 | tf_op jit(solution)/shard_map/mul | solution.py:201
  27.9 0.0 copy-done.6
  28.0 0.1 dynamic-slice_bitcast_fusion
  28.0 0.0 copy-done.7
  28.0 0.1 select_reduce_fusion
  28.2 0.2 fusion.1
  28.3 0.0 collective-permute-done.2.fourth_ref
  28.4 0.0 copy-start.2
  28.4 6.6 %collective-permute-start.3 = (bf16[2,128,512]{2,1,0:T(8,128)(2,1)S(1)}, bf16[2,128,512]{2,1,0:T(8,128)(2,1)S(1)}, u32[]{:S(2)}, u32[]{:S(2)}) collective-permute-start(bf16[2,128,512]{2,1,0:T(8,128)(2,1)S(1)} %collective-permute-done.2.fourth_ref), channel_id=1, source_target_pairs={{0,31},{1,0},{2,1},{3,2},{4,3},{5,4},{6,5},{7,6},{8,7},{9,8},{10,9... | collective-permute-start | bytes 786440 | tf_op jit(solution)/shard_map/ppermute | solution.py:193
  34.9 0.0 collective-permute-done.near_ref
  34.9 0.0 copy-start.3
  34.9 1.9 %collective-permute-start.1 = (bf16[2,128,512]{2,1,0:T(8,128)(2,1)S(1)}, bf16[2,128,512]{2,1,0:T(8,128)(2,1)S(1)}, u32[]{:S(2)}, u32[]{:S(2)}) collective-permute-start(bf16[2,128,512]{2,1,0:T(8,128)(2,1)S(1)} %collective-permute-done.near_ref), channel_id=1, source_target_pairs={{0,1},{1,2},{2,3},{3,4},{4,5},{5,6},{6,7},{7,8},{8,9},{9,10},{10,1... | collective-permute-start | bytes 786440 | tf_op jit(solution)/shard_map/ppermute | solution.py:193
  36.9 0.1 fusion.3.back_ref
  36.9 0.0 all-to-all-done
  36.9 0.6 slice_reduce_fusion
  37.6 1.1 %collective-permute-done.3.far_ref = bf16[2,128,512]{2,1,0:T(8,128)(2,1)S(1)} collective-permute-done((bf16[2,128,512]{2,1,0:T(8,128)(2,1)S(1)}, bf16[2,128,512]{2,1,0:T(8,128)(2,1)S(1)}, u32[]{:S(2)}, u32[]{:S(2)}) %collective-permute-start.3) | collective-permute-done | bytes 262176 | tf_op jit(solution)/shard_map/ppermute | solution.py:193
  38.7 0.0 copy-start.4
  38.7 7.2 %collective-permute-done.1.mid_ref = bf16[2,128,512]{2,1,0:T(8,128)(2,1)S(1)} collective-permute-done((bf16[2,128,512]{2,1,0:T(8,128)(2,1)S(1)}, bf16[2,128,512]{2,1,0:T(8,128)(2,1)S(1)}, u32[]{:S(2)}, u32[]{:S(2)}) %collective-permute-start.1) | collective-permute-done | bytes 262176 | tf_op jit(solution)/shard_map/ppermute | solution.py:193
  45.9 0.0 copy-done.2
  45.9 0.0 copy-done.3
  45.9 0.0 copy-done.4
  45.9 0.0 copy-start.5
  45.9 0.7 copy-done.5
  46.6 0.0 copy-done
  46.6 11.5 %attention.1 = (bf16[128,4096]{1,0:T(8,128)(2,1)}, bf16[128,4096]{1,0:T(8,128)(2,1)S(1)}, f32[2,128,512]{2,1,0:T(8,128)}, bf16[2,128,512]{2,1,0:T(8,128)(2,1)S(1...) custom-call(s32[2]{0:T(128)S(1)} %fusion.3.back_ref, ...), custom_call_target="tpu_custom_call" | custom-call | tf_op jit(solution)/shard_map/attention/pallas_call | solution.py:143
  58.1 0.0 copy-start.1
  58.1 2.0 %collective-permute-start.4 = (bf16[2,128,512]{2,1,0:T(8,128)(2,1)S(1)}, bf16[2,128,512]{2,1,0:T(8,128)(2,1)S(1)}, u32[]{:S(2)}, u32[]{:S(2)}) collective-permute-start(bf16[2,128,512]{2,1,0:T(8,128)(2,1)S(1)} %get-tuple-element.18), channel_id=1, source_target_pairs={{0,31},{1,0},{2,1},{3,2},{4,3},{5,4},{6,5},{7,6},{8,7},{9,8},{10,9... | collective-permute-start | bytes 786440 | tf_op jit(solution)/shard_map/ppermute | solution.py:193
  60.2 3.4 %collective-permute-start.5 = (bf16[2,128,512]{2,1,0:T(8,128)(2,1)S(1)}, bf16[2,128,512]{2,1,0:T(8,128)(2,1)S(1)}, u32[]{:S(2)}, u32[]{:S(2)}) collective-permute-start(bf16[2,128,512]{2,1,0:T(8,128)(2,1)S(1)} %get-tuple-element.20), channel_id=1, source_target_pairs={{0,1},{1,2},{2,3},{3,4},{4,5},{5,6},{6,7},{7,8},{8,9},{9,10},{10,1... | collective-permute-start | bytes 786440 | tf_op jit(solution)/shard_map/ppermute | solution.py:193
  63.5 1.8 %collective-permute-done.4 = bf16[2,128,512]{2,1,0:T(8,128)(2,1)S(1)} collective-permute-done((bf16[2,128,512]{2,1,0:T(8,128)(2,1)S(1)}, bf16[2,128,512]{2,1,0:T(8,128)(2,1)S(1)}, u32[]{:S(2)}, u32[]{:S(2)}) %collective-permute-start.4) | collective-permute-done | bytes 262176 | tf_op jit(solution)/shard_map/ppermute | solution.py:193
  65.4 0.1 add.16
  65.4 5.2 %collective-permute-start.6 = (bf16[2,128,512]{2,1,0:T(8,128)(2,1)S(1)}, bf16[2,128,512]{2,1,0:T(8,128)(2,1)S(1)}, u32[]{:S(2)}, u32[]{:S(2)}) collective-permute-start(bf16[2,128,512]{2,1,0:T(8,128)(2,1)S(1)} %add.16), channel_id=1, source_target_pairs={{0,31},{1,0},{2,1},{3,2},{4,3},{5,4},{6,5},{7,6},{8,7},{9,8},{10,9... | collective-permute-start | bytes 786440 | tf_op jit(solution)/shard_map/ppermute | solution.py:193
  70.7 0.0 collective-permute-done.5
  70.7 0.1 add.17
  70.8 5.2 %collective-permute-start.7 = (bf16[2,128,512]{2,1,0:T(8,128)(2,1)S(1)}, bf16[2,128,512]{2,1,0:T(8,128)(2,1)S(1)}, u32[]{:S(2)}, u32[]{:S(2)}) collective-permute-start(bf16[2,128,512]{2,1,0:T(8,128)(2,1)S(1)} %add.17), channel_id=1, source_target_pairs={{0,28},{1,29},{2,30},{3,31},{4,0},{5,1},{6,2},{7,3},{8,4},{9,5},{1... | collective-permute-start | bytes 786440 | tf_op jit(solution)/shard_map/ppermute | solution.py:193
  76.0 0.7 broadcast_in_dim.48
  76.6 16.6 %all_to_all.10 = f32[16,1,128]{2,1,0:T(1,128)S(1)} all-to-all(f32[16,1,128]{2,1,0:T(1,128)S(1)} %broadcast_in_dim.48), channel_id=1, replica_groups=mesh['dp'=16,'ctx'=32] {'dp'}, dimensions={0} | all-to-all | bytes 16384 | tf_op jit(solution)/shard_map/all_to_all | solution.py:177
  93.2 0.6 slice_reduce_fusion.1
  93.9 0.0 collective-permute-done.6
  93.9 0.0 collective-permute-done.7
  93.9 0.0 copy-done.1
  93.9 0.1 convert_add_fusion
  94.7 1.2 %fusion = bf16[1,128,4096]{2,1,0:T(8,128)(2,1)} fusion(bf16[128,4096]{1,0:T(8,128)(2,1)S(1)} %get-tuple-element.16, f32[]{:T(128)S(6)} %div.3), kind=kLoop, calls=%fused_computation.1 | loop fusion | flops 1572864 | bytes 2097156 | tf_op jit(solution)/shard_map/broadcast_in_dim | solution.py:219
  95.9 0.7 fusion.2
  (1 shorter events, 0.0 us)
Async XLA Ops:
  2.5 25.9 %collective-permute-start.2 = (bf16[2,128,512]{2,1,0:T(8,128)(2,1)S(1)}, bf16[2,128,512]{2,1,0:T(8,128)(2,1)S(1)}, u32[]{:S(2)}, u32[]{:S(2)}) collective-permute-start(bf16[2,128,512]{2,1,0:T(8,128)(2,1)S(1)} %constant_dynamic-update-slice_fusion.own_ref), channel_id=1, source_target_pairs={{0,4},{1,5},{2,6},{3,7},{4,8},{5,9},{6,10},{7,11},{8,12},{9,13},{1... | collective-permute-start | bytes 786440 | tf_op jit(solution)/shard_map/ppermute | solution.py:193
  13.9 21.0 %collective-permute-start = (bf16[2,128,512]{2,1,0:T(8,128)(2,1)S(1)}, bf16[2,128,512]{2,1,0:T(8,128)(2,1)S(1)}, u32[]{:S(2)}, u32[]{:S(2)}) collective-permute-start(bf16[2,128,512]{2,1,0:T(8,128)(2,1)S(1)} %constant_dynamic-update-slice_fusion.own_ref), channel_id=1, source_target_pairs={{0,1},{1,2},{2,3},{3,4},{4,5},{5,6},{6,7},{7,8},{8,9},{9,10},{10,1... | collective-permute-start | bytes 786440 | tf_op jit(solution)/shard_map/ppermute | solution.py:193
  19.6 17.4 %all-to-all-start = ((f32[32,1,128]{2,1,0:T(1,128)}), f32[32,1,128]{2,1,0:T(1,128)S(1)}, u32[]{:S(2)}, u32[]{:S(2)}) async-start(f32[32,1,128]{2,1,0:T(1,128)} %broadcast_in_dim.46), calls=%async_computation | async-start | bytes 32768 | tf_op jit(solution)/shard_map/all_to_all | solution.py:177
  26.5 1.5 %copy-start.6 = (s32[1,64]{1,0:T(1,128)S(1)}, s32[1,64]{1,0:T(1,128)}, u32[]{:S(2)}) copy-start(s32[1,64]{1,0:T(1,128)} %param.12) | copy-start | bytes 772
  26.5 1.5 %copy-start.7 = (s32[1,21]{1,0:T(1,128)S(1)}, s32[1,21]{1,0:T(1,128)}, u32[]{:S(2)}) copy-start(s32[1,21]{1,0:T(1,128)} %param.11) | copy-start | bytes 256
  26.5 20.1 %copy-start = (bf16[1,128,4096]{2,1,0:T(8,128)(2,1)S(1)}, bf16[1,128,4096]{2,1,0:T(8,128)(2,1)}, u32[]{:S(2)}) copy-start(bf16[1,128,4096]{2,1,0:T(8,128)(2,1)} %param.7) | copy-start | bytes 3145732
  28.4 17.5 %copy-start.2 = (bf16[2,128,512]{2,1,0:T(8,128)(2,1)}, bf16[2,128,512]{2,1,0:T(8,128)(2,1)S(1)}, u32[]{:S(2)}) copy-start(bf16[2,128,512]{2,1,0:T(8,128)(2,1)S(1)} %collective-permute-done.2.fourth_ref) | copy-start | bytes 786436
  28.4 10.3 %collective-permute-start.3 = (bf16[2,128,512]{2,1,0:T(8,128)(2,1)S(1)}, bf16[2,128,512]{2,1,0:T(8,128)(2,1)S(1)}, u32[]{:S(2)}, u32[]{:S(2)}) collective-permute-start(bf16[2,128,512]{2,1,0:T(8,128)(2,1)S(1)} %collective-permute-done.2.fourth_ref), channel_id=1, source_target_pairs={{0,31},{1,0},{2,1},{3,2},{4,3},{5,4},{6,5},{7,6},{8,7},{9,8},{10,9... | collective-permute-start | bytes 786440 | tf_op jit(solution)/shard_map/ppermute | solution.py:193
  34.9 10.9 %copy-start.3 = (bf16[2,128,512]{2,1,0:T(8,128)(2,1)}, bf16[2,128,512]{2,1,0:T(8,128)(2,1)S(1)}, u32[]{:S(2)}) copy-start(bf16[2,128,512]{2,1,0:T(8,128)(2,1)S(1)} %collective-permute-done.near_ref) | copy-start | bytes 786436
  34.9 10.9 %collective-permute-start.1 = (bf16[2,128,512]{2,1,0:T(8,128)(2,1)S(1)}, bf16[2,128,512]{2,1,0:T(8,128)(2,1)S(1)}, u32[]{:S(2)}, u32[]{:S(2)}) collective-permute-start(bf16[2,128,512]{2,1,0:T(8,128)(2,1)S(1)} %collective-permute-done.near_ref), channel_id=1, source_target_pairs={{0,1},{1,2},{2,3},{3,4},{4,5},{5,6},{6,7},{7,8},{8,9},{9,10},{10,1... | collective-permute-start | bytes 786440 | tf_op jit(solution)/shard_map/ppermute | solution.py:193
  38.7 7.2 %copy-start.4 = (bf16[2,128,512]{2,1,0:T(8,128)(2,1)}, bf16[2,128,512]{2,1,0:T(8,128)(2,1)S(1)}, u32[]{:S(2)}) copy-start(bf16[2,128,512]{2,1,0:T(8,128)(2,1)S(1)} %collective-permute-done.3.far_ref) | copy-start | bytes 786436
  45.9 0.7 copy-start.5
  58.1 35.7 %copy-start.1 = (f32[2,128,512]{2,1,0:T(8,128)S(1)}, f32[2,128,512]{2,1,0:T(8,128)}, u32[]{:S(2)}) copy-start(f32[2,128,512]{2,1,0:T(8,128)} %get-tuple-element.22) | copy-start | bytes 1572868
  58.1 7.2 %collective-permute-start.4 = (bf16[2,128,512]{2,1,0:T(8,128)(2,1)S(1)}, bf16[2,128,512]{2,1,0:T(8,128)(2,1)S(1)}, u32[]{:S(2)}, u32[]{:S(2)}) collective-permute-start(bf16[2,128,512]{2,1,0:T(8,128)(2,1)S(1)} %get-tuple-element.18), channel_id=1, source_target_pairs={{0,31},{1,0},{2,1},{3,2},{4,3},{5,4},{6,5},{7,6},{8,7},{9,8},{10,9... | collective-permute-start | bytes 786440 | tf_op jit(solution)/shard_map/ppermute | solution.py:193
  60.2 10.5 %collective-permute-start.5 = (bf16[2,128,512]{2,1,0:T(8,128)(2,1)S(1)}, bf16[2,128,512]{2,1,0:T(8,128)(2,1)S(1)}, u32[]{:S(2)}, u32[]{:S(2)}) collective-permute-start(bf16[2,128,512]{2,1,0:T(8,128)(2,1)S(1)} %get-tuple-element.20), channel_id=1, source_target_pairs={{0,1},{1,2},{2,3},{3,4},{4,5},{5,6},{6,7},{7,8},{8,9},{9,10},{10,1... | collective-permute-start | bytes 786440 | tf_op jit(solution)/shard_map/ppermute | solution.py:193
  65.4 28.4 %collective-permute-start.6 = (bf16[2,128,512]{2,1,0:T(8,128)(2,1)S(1)}, bf16[2,128,512]{2,1,0:T(8,128)(2,1)S(1)}, u32[]{:S(2)}, u32[]{:S(2)}) collective-permute-start(bf16[2,128,512]{2,1,0:T(8,128)(2,1)S(1)} %add.16), channel_id=1, source_target_pairs={{0,31},{1,0},{2,1},{3,2},{4,3},{5,4},{6,5},{7,6},{8,7},{9,8},{10,9... | collective-permute-start | bytes 786440 | tf_op jit(solution)/shard_map/ppermute | solution.py:193
  70.8 23.1 %collective-permute-start.7 = (bf16[2,128,512]{2,1,0:T(8,128)(2,1)S(1)}, bf16[2,128,512]{2,1,0:T(8,128)(2,1)S(1)}, u32[]{:S(2)}, u32[]{:S(2)}) collective-permute-start(bf16[2,128,512]{2,1,0:T(8,128)(2,1)S(1)} %add.17), channel_id=1, source_target_pairs={{0,28},{1,29},{2,30},{3,31},{4,0},{5,1},{6,2},{7,3},{8,4},{9,5},{1... | collective-permute-start | bytes 786440 | tf_op jit(solution)/shard_map/ppermute | solution.py:193

commit v3 on v2

v3 whole, which is shorter than its diff:
```python
import math

import jax
import jax.numpy as jnp
from jax import lax
from jax.experimental import pallas as pl
from jax.experimental.pallas import tpu as pltpu
from jax.sharding import PartitionSpec as P

HEAD_WIDTH = 128
QUERY_HEADS = 32
KEY_VALUE_HEADS = 4
ALIGN_TOKENS = 64
MOST = 8
PACK_TOKENS = 4096
GROUP = QUERY_HEADS // KEY_VALUE_HEADS
SPAN = MOST * ALIGN_TOKENS
LOG2E = math.log2(math.e)
SCALE = 1.0 / math.sqrt(HEAD_WIDTH)
HIDDEN = -1e30
QUERY_PIECES = 4


def dot_nt(a, b):
    return lax.dot_general(a, b, (((1,), (1,)), ((), ())), preferred_element_type=jnp.float32)


def dot_nn(a, b):
    return lax.dot_general(a, b, (((1,), (0,)), ((), ())), preferred_element_type=jnp.float32)


def dot_tn(a, b):
    return lax.dot_general(a, b, (((0,), (0,)), ((), ())), preferred_element_type=jnp.float32)


def fold_rows(x, op):
    folded = x[:8]
    for i in range(8, x.shape[0], 8):
        folded = op(folded, x[i : i + 8])
    return folded


def attention_kernel(
    back_ref,
    q_ref,
    g_ref,
    own_ref,
    near_ref,
    mid_ref,
    far_ref,
    fourth_ref,
    out_ref,
    dq_ref,
    own_part,
    near_part,
    mid_part,
    far_part,
    fourth_part,
    keys_acc,
    values_acc,
):
    width, block = HEAD_WIDTH, ALIGN_TOKENS
    group = GROUP * width
    shards_in = (fourth_ref, far_ref, mid_ref, near_ref, own_ref)
    tokens = own_ref.shape[1]
    rows, count, cols = len(shards_in) * tokens, tokens // block, GROUP * block
    causal = lax.broadcasted_iota(jnp.int32, (block, cols), 0) <= (
        lax.broadcasted_iota(jnp.int32, (block, cols), 1) & (block - 1)
    )

    def stacked(ref, k, t):
        at, first = slice(t * block, (t + 1) * block), k * GROUP
        return [
            ref[at, h * width : (h + 1) * width] for h in range(first, first + GROUP)
        ]

    def query_rows(k, t):
        return jnp.concatenate(stacked(q_ref, k, t), axis=0)

    def grad_rows(k, t):
        return jnp.concatenate(stacked(g_ref, k, t), axis=0)

    def halo(k, side):
        at = slice(k * width, (k + 1) * width)
        return jnp.concatenate([ref[side, :, at] for ref in shards_in], axis=0)

    def window(t):
        lo = rows - SPAN - (count - 1 - t) * block
        return slice(lo, lo + SPAN)

    def probabilities(t, s, dp):
        hidden = [jnp.where(b >= MOST - 1 - back_ref[t], 0.0, HIDDEN) for b in range(MOST - 1)]
        hidden.append(0.0)
        s = [s[b * block : (b + 1) * block] for b in range(MOST)]
        s[-1] = jnp.where(causal, s[-1], HIDDEN)
        dp = [dp[b * block : (b + 1) * block] for b in range(MOST)]
        peak = None
        for b in range(MOST):
            part = fold_rows(s[b], jnp.maximum) + hidden[b]
            peak = part if peak is None else jnp.maximum(peak, part)
        peak = jnp.max(peak, axis=0, keepdims=True)
        e, total, weighed = [], None, None
        for b in range(MOST):
            e.append(jnp.exp2((s[b] - (peak - hidden[b])) * (SCALE * LOG2E)))
            part, part_weighed = fold_rows(e[b], jnp.add), fold_rows(e[b] * dp[b], jnp.add)
            total = part if total is None else total + part
            weighed = part_weighed if weighed is None else weighed + part_weighed
        inverse = 1.0 / jnp.sum(total, axis=0, keepdims=True)
        delta = jnp.sum(weighed, axis=0, keepdims=True) * inverse
        p_low, ds = [], []
        for b in range(MOST):
            p = e[b] * inverse
            p_low.append(p.astype(jnp.bfloat16))
            ds.append((p * (dp[b] - delta)).astype(jnp.bfloat16))
        return jnp.concatenate(p_low, axis=0), jnp.concatenate(ds, axis=0)

    def products(k, t, keys, values):
        return (
            dot_nt(keys[window(t)], query_rows(k, t)),
            dot_nt(values[window(t)], grad_rows(k, t)),
        )

    steps = [(k, t) for k in range(KEY_VALUE_HEADS) for t in range(count)]
    sides = {k: (halo(k, 0), halo(k, 1)) for k in range(KEY_VALUE_HEADS)}
    ahead = products(*steps[0], *sides[0])
    for n, (k, t) in enumerate(steps):
        now = ahead
        if n + 1 < len(steps):
            ahead = products(*steps[n + 1], *sides[steps[n + 1][0]])
        if t == 0:
            keys_acc[...] = jnp.zeros_like(keys_acc)
            values_acc[...] = jnp.zeros_like(values_acc)
        keys, values = sides[k]
        p_low, ds = probabilities(t, *now)
        keys_acc[window(t), :] += dot_nn(ds, query_rows(k, t))
        values_acc[window(t), :] += dot_nn(p_low, grad_rows(k, t))
        out = dot_tn(p_low, values[window(t)]).astype(jnp.bfloat16)
        dq = (dot_tn(ds, keys[window(t)]) * SCALE).astype(jnp.bfloat16)
        place = (slice(t * block, (t + 1) * block), slice(k * group, (k + 1) * group))
        for ref, heads in ((out_ref, out), (dq_ref, dq)):
            ref[place] = jnp.concatenate(
                [heads[h * block : (h + 1) * block] for h in range(GROUP)], axis=1
            )
        if t == count - 1:
            at = slice(k * width, (k + 1) * width)
            for i, ref in enumerate((fourth_part, far_part, mid_part, near_part, own_part)):
                part = slice(i * tokens, (i + 1) * tokens)
                ref[0, :, at] = (keys_acc[part, :] * SCALE).astype(ref.dtype)
                ref[1, :, at] = values_acc[part, :].astype(ref.dtype)


def attention(back, queries, grads, halo):
    tokens = queries.shape[0]
    whole = pl.BlockSpec(memory_space=pltpu.VMEM)
    shape = jax.ShapeDtypeStruct
    return pl.pallas_call(
        attention_kernel,
        in_specs=[pl.BlockSpec(memory_space=pltpu.SMEM)] + [whole] * 7,
        out_specs=[whole] * 7,
        scratch_shapes=[pltpu.VMEM((5 * tokens, HEAD_WIDTH), jnp.float32)] * 2,
        out_shape=[shape(queries.shape, jnp.bfloat16)] * 2
        + [shape(halo[0].shape, jnp.float32)]
        + [shape(halo[0].shape, jnp.bfloat16)] * 4,
        compiler_params=pltpu.CompilerParams(vmem_limit_bytes=40 * 1024 * 1024),
        name="attention",
    )(back, queries, grads, *halo)


def total_kernel(rows_ref, out_ref):
    rows = rows_ref[...].astype(jnp.float32)
    first = lax.broadcasted_iota(jnp.int32, rows.shape, rows.ndim - 1) == 0
    if rows.shape[0] > 1:
        rows = jnp.where(first, rows, 0.0)
    out_ref[...] = jnp.full(out_ref.shape, jnp.sum(rows), jnp.float32)


def kept_kernel(mask_ref, grads_ref, kept_ref):
    tokens, width = mask_ref.shape[1], HEAD_WIDTH
    mask = jnp.broadcast_to(mask_ref[...].astype(jnp.float32), (width, tokens))
    mask = jnp.transpose(mask).astype(jnp.bfloat16)
    for h in range(grads_ref.shape[1] // width):
        at = slice(h * width, (h + 1) * width)
        kept_ref[:, at] = grads_ref[:, at] * mask


def kept_grads(mask, grads):
    columns = pl.BlockSpec((grads.shape[0], GROUP * HEAD_WIDTH), lambda i: (0, i))
    return pl.pallas_call(
        kept_kernel,
        grid=(KEY_VALUE_HEADS,),
        in_specs=[pl.BlockSpec(mask.shape, lambda i: (0, 0)), columns],
        out_specs=columns,
        out_shape=jax.ShapeDtypeStruct(grads.shape, grads.dtype),
        cost_estimate=pl.CostEstimate(flops=0, bytes_accessed=0, transcendentals=0),
        name="kept_grads",
    )(mask, grads)


def spread_total(rows, copies, space=None):
    return pl.pallas_call(
        total_kernel,
        in_specs=[pl.BlockSpec(memory_space=space)],
        out_shape=jax.ShapeDtypeStruct((copies, 1, HEAD_WIDTH), jnp.float32),
        name="spread_total",
    )(rows)


def gradients_kernel(
    rows_ref,
    dq_ref,
    own_ref,
    near_ref,
    fourth_ref,
    grad_queries_ref,
    grad_keys_ref,
    grad_values_ref,
    queries_out,
    sides_out,
    sems,
):
    tokens_in_all = rows_ref.shape[0] * PACK_TOKENS
    first = lax.broadcasted_iota(jnp.int32, rows_ref.shape, 2) == 0
    factor = tokens_in_all / jnp.sum(jnp.where(first, rows_ref[...], 0.0))
    copies = []
    rows = dq_ref.shape[0] // QUERY_PIECES
    for i in range(QUERY_PIECES):
        at = slice(i * rows, (i + 1) * rows)
        queries_out[at] = (dq_ref[at].astype(jnp.float32) * factor).astype(jnp.bfloat16)
        copies.append(
            pltpu.make_async_copy(queries_out.at[at], grad_queries_ref.at[at], sems.at[i])
        )
        copies[-1].start()
    for side, ref in enumerate((grad_keys_ref, grad_values_ref)):
        back = near_ref[side].astype(jnp.float32) + fourth_ref[side].astype(jnp.float32)
        sides_out[side] = ((own_ref[side] + back) * factor).astype(jnp.bfloat16)
        copies.append(
            pltpu.make_async_copy(sides_out.at[side], ref, sems.at[QUERY_PIECES + side])
        )
        copies[-1].start()
    for copy in copies:
        copy.wait()


def gradients(rows, dq, own_part, near_back, fourth_back):
    narrow = jax.ShapeDtypeStruct(own_part.shape[1:], jnp.bfloat16)
    return pl.pallas_call(
        gradients_kernel,
        in_specs=[pl.BlockSpec(memory_space=pltpu.VMEM)] * 5,
        out_specs=[pl.BlockSpec(memory_space=pltpu.HBM)] * 3,
        out_shape=[jax.ShapeDtypeStruct(dq.shape, jnp.bfloat16), narrow, narrow],
        scratch_shapes=[
            pltpu.VMEM(dq.shape, jnp.bfloat16),
            pltpu.VMEM(own_part.shape, jnp.bfloat16),
            pltpu.SemaphoreType.DMA((QUERY_PIECES + 2,)),
        ],
        compiler_params=pltpu.CompilerParams(vmem_limit_bytes=24 * 1024 * 1024),
        name="gradients",
    )(rows, dq, own_part, near_back, fourth_back)


def exchanged(rows, axis):
    return lax.all_to_all(rows, axis, split_axis=0, concat_axis=0)


def blocks_back(lengths, order, first, count):
    ends = jnp.sum(
        jnp.where(
            jnp.arange(lengths.shape[0])[:, None] >= jnp.arange(lengths.shape[0])[None, :],
            lengths[None, :],
            0,
        ),
        axis=1,
    )
    places = lax.dynamic_slice_in_dim(order, first, count, 0)
    starts = jnp.max(jnp.where(ends[None, :] <= places[:, None], ends[None, :], 0), axis=1)
    return places - starts


def after(value, *others):
    return lax.optimization_barrier((value, *others))[0]


def shards(
    queries, key_head_states, value_head_states, out_grad, doc_blocks, block_order, target_mask
):
    tokens = queries.shape[1]
    ctx_count = lax.axis_size("ctx")

    def shift(array, steps):
        pairs = [(i, (i + steps) % ctx_count) for i in range(ctx_count)]
        return lax.ppermute(array, "ctx", pairs)

    side = lax.broadcasted_iota(jnp.int32, (2, 1, 1), 0)
    own = jnp.where(side == 0, key_head_states, value_head_states)
    fourth = shift(own, 4)
    near = shift(own, 1)
    counts = exchanged(spread_total(target_mask, ctx_count), "ctx")
    mid = shift(near, 1)
    far = shift(fourth, -1)
    pack_counts = spread_total(counts, lax.axis_size("dp"), pltpu.VMEM)
    blocks = tokens // ALIGN_TOKENS
    back = blocks_back(doc_blocks[0], block_order[0], lax.axis_index("ctx") * blocks, blocks)
    back = after(back, pack_counts)
    grads = kept_grads(after(target_mask, near, fourth), out_grad[0])
    attended, dq, own_part, near_part, mid_part, far_part, fourth_part = attention(
        back, queries[0], grads, (own, near, mid, far, fourth)
    )
    mid_back = shift(mid_part, -1)
    far_on = shift(far_part, 1)
    near_sum = near_part + mid_back
    fourth_sum = fourth_part + far_on
    fourth_back = shift(fourth_sum, -4)
    near_back = shift(near_sum, -1)
    counts = exchanged(after(pack_counts, near_sum, fourth_sum), "dp")
    grad_queries, grad_keys, grad_values = gradients(counts, dq, own_part, near_back, fourth_back)
    return (attended[None], grad_queries[None], grad_keys[None], grad_values[None])


def solution(mesh):
    placed = (
        P("dp", "ctx", None),
        P("dp", "ctx", None),
        P("dp", "ctx", None),
        P("dp", "ctx", None),
        P("dp", None),
        P("dp", None),
        P("dp", "ctx"),
    )
    return jax.shard_map(
        shards,
        mesh=mesh,
        in_specs=placed,
        out_specs=(
            P("dp", "ctx", None),
            P("dp", "ctx", None),
            P("dp", "ctx", None),
            P("dp", "ctx", None),
        ),
        check_vma=False,
    )
```

time: 97.2 us -> 92.6 us (0.953)
  Pallas kernels: 11.5 us -> 17.6 us
  other arithmetic: 6.46 us -> 1.57 us
  local copies, waits for them, and re-layouts: 5.25 us -> 3.22 us
  waiting for transfers between devices: 10.1 us -> 8.59 us
  starting transfers between devices: 45.1 us -> 43.8 us
    pallas_call x1 -> x5, Pallas kernels: 11.5 us -> 17.6 us  [the longest x1 9.8 us: attention(): pl.pallas_call(attention_kernel, in_specs=[pl.BlockSpec(memory_space=pltp...]
    reduce_sum x3 -> x0, other arithmetic: 2.51 us -> none  [the longest x1 1.26 us: shards(): pack_total = axis_total(jnp.sum(target_mask.astype(jnp.float32)), 'ctx')]
    broadcast_in_dim x2 -> x0, local copies, waits for them, and re-layouts: 1.91 us -> none  [axis_total(): sent = jnp.broadcast_to(value, (n, 1, HEAD_WIDTH))]
    ppermute x8, waiting for transfers between devices: 10.1 us -> 8.59 us  [shift(): return lax.ppermute(array, 'ctx', pairs)]
    unnamed x17 -> x12, local copies, waits for them, and re-layouts: 1.63 us -> 3.15 us
    mul x1 -> x0, other arithmetic: 1.45 us -> none  [shards(): grads = out_grad[0] * target_mask[0].astype(jnp.bfloat16)[:, None]]
    ppermute x8, starting transfers between devices: 38.9 us -> 37.6 us  [shift(): return lax.ppermute(array, 'ctx', pairs)]
    broadcast_in_dim x1 -> x0, other arithmetic: 1.18 us -> none  [shards(): return (attended[None], grad_queries[None], whole[:1], whole[1:])]
  transfers between devices with their start and end apart: 9 -> 9, of which waited for: 3 -> 3; matrix products, arithmetic and copies ran while one was open for 7% -> 1% of each run, Pallas kernels for 0% -> 7%
where the time goes in v3:
time: 92.6 us; the launch traced here: 92 us
  starting transfers between devices  43.8 us (47%)
  Pallas kernels  17.6 us (19%)
  blocking collectives  16.4 us (18%)
  waiting for transfers between devices  8.59 us (9%)
  local copies, waits for them, and re-layouts  3.22 us (3%)
  other arithmetic  1.57 us (2%)
    ppermute x8, starting transfers between devices, shift(): return lax.ppermute(array, 'ctx', pairs)  37.6 us
    all_to_all x1, blocking collectives, exchanged(): return lax.all_to_all(rows, axis, split_axis=0, concat_axis=0)  16.4 us
    pallas_call x1, Pallas kernels, attention(): pl.pallas_call(attention_kernel, in_specs=[pl.BlockSpec(memory_space=pltp...  9.8 us
    ppermute x8, waiting for transfers between devices, shift(): return lax.ppermute(array, 'ctx', pairs)  8.59 us
    all_to_all x1, starting transfers between devices, exchanged(): return lax.all_to_all(rows, axis, split_axis=0, concat_axis=0)  6.24 us
    pallas_call x1, Pallas kernels, kept_grads(): pl.pallas_call(kept_kernel, grid=(KEY_VALUE_HEADS,), in_specs=[pl.BlockSp...  3.63 us
    unnamed x12, local copies, waits for them, and re-layouts  3.15 us
    pallas_call x2, Pallas kernels, spread_total(): pl.pallas_call(total_kernel, in_specs=[pl.BlockSpec(memory_space=space)],...  2.86 us
  transfers between devices with their start and end apart: 9, of which 3 were waited for; matrix products, arithmetic and copies ran while one was open for 1% of the time, Pallas kernels for 7%

profile of v3, /device:TPU:1, one launch (start us, length us, event | category | flops | bytes accessed | tf_op | source)
XLA Modules:
  0.0 92.0 jit_solution(5560730265705923453)
XLA Ops:
  0.6 1.1 %broadcast_select_fusion.own_ref = bf16[2,128,512]{2,1,0:T(8,128)(2,1)S(1)} fusion(pred[2]{0:T(512)(128)(4,1)S(1)} %iota_compare_fusion.1, bf16[128,512]{1,0:T(8,128)(2,1)} %bitcast.15, bf16[128,512]{1,0:T(8,128)(2,1)} %bitcast.16), kind=kLoop, calls=%fused_computation | loop fusion | flops 131072 | bytes 524290 | tf_op jit(solution)/shard_map/jit(_where)/select_n | solution.py:294
  1.7 11.5 %collective-permute-start.1 = (bf16[2,128,512]{2,1,0:T(8,128)(2,1)S(1)}, bf16[2,128,512]{2,1,0:T(8,128)(2,1)S(1)}, u32[]{:S(2)}, u32[]{:S(2)}) collective-permute-start(bf16[2,128,512]{2,1,0:T(8,128)(2,1)S(1)} %broadcast_select_fusion.own_ref), channel_id=1, source_target_pairs={{0,4},{1,5},{2,6},{3,7},{4,8},{5,9},{6,10},{7,11},{8,12},{9,13},{1... | collective-permute-start | bytes 786440 | tf_op jit(solution)/shard_map/ppermute | solution.py:291
  13.2 3.1 %collective-permute-start = (bf16[2,128,512]{2,1,0:T(8,128)(2,1)S(1)}, bf16[2,128,512]{2,1,0:T(8,128)(2,1)S(1)}, u32[]{:S(2)}, u32[]{:S(2)}) collective-permute-start(bf16[2,128,512]{2,1,0:T(8,128)(2,1)S(1)} %broadcast_select_fusion.own_ref), channel_id=1, source_target_pairs={{0,1},{1,2},{2,3},{3,4},{4,5},{5,6},{6,7},{7,8},{8,9},{9,10},{10,1... | collective-permute-start | bytes 786440 | tf_op jit(solution)/shard_map/ppermute | solution.py:291
  16.3 1.4 %spread_total.2 = f32[32,1,128]{2,1,0:T(1,128)} custom-call(s32[1,128]{1,0:T(1,128)} %mask_ref), custom_call_target="tpu_custom_call" | custom-call | tf_op jit(solution)/shard_map/spread_total/pallas_call | solution.py:200
  17.7 6.2 %all-to-all-start = ((f32[32,1,128]{2,1,0:T(1,128)}), f32[32,1,128]{2,1,0:T(1,128)S(1)}, u32[]{:S(2)}, u32[]{:S(2)}) async-start(f32[32,1,128]{2,1,0:T(1,128)} %spread_total.2), calls=%async_computation | async-start | bytes 32768 | tf_op jit(solution)/shard_map/all_to_all | solution.py:262
  23.9 0.0 copy-start.4
  23.9 0.6 copy-done.4
  24.6 0.1 dynamic-slice_bitcast_fusion
  24.7 0.0 copy-start.5
  24.7 0.7 copy-done.5
  25.3 0.1 select_reduce_fusion
  25.4 0.0 collective-permute-done.1.fourth_ref
  25.4 6.6 %collective-permute-start.3 = (bf16[2,128,512]{2,1,0:T(8,128)(2,1)S(1)}, bf16[2,128,512]{2,1,0:T(8,128)(2,1)S(1)}, u32[]{:S(2)}, u32[]{:S(2)}) collective-permute-start(bf16[2,128,512]{2,1,0:T(8,128)(2,1)S(1)} %collective-permute-done.1.fourth_ref), channel_id=1, source_target_pairs={{0,31},{1,0},{2,1},{3,2},{4,3},{5,4},{6,5},{7,6},{8,7},{9,8},{10,9... | collective-permute-start | bytes 786440 | tf_op jit(solution)/shard_map/ppermute | solution.py:291
  32.0 1.4 %collective-permute-done.near_ref = bf16[2,128,512]{2,1,0:T(8,128)(2,1)S(1)} collective-permute-done((bf16[2,128,512]{2,1,0:T(8,128)(2,1)S(1)}, bf16[2,128,512]{2,1,0:T(8,128)(2,1)S(1)}, u32[]{:S(2)}, u32[]{:S(2)}) %collective-permute-start) | collective-permute-done | bytes 262176 | tf_op jit(solution)/shard_map/ppermute | solution.py:291
  33.4 1.9 %collective-permute-start.2 = (bf16[2,128,512]{2,1,0:T(8,128)(2,1)S(1)}, bf16[2,128,512]{2,1,0:T(8,128)(2,1)S(1)}, u32[]{:S(2)}, u32[]{:S(2)}) collective-permute-start(bf16[2,128,512]{2,1,0:T(8,128)(2,1)S(1)} %collective-permute-done.near_ref), channel_id=1, source_target_pairs={{0,1},{1,2},{2,3},{3,4},{4,5},{5,6},{6,7},{7,8},{8,9},{9,10},{10,1... | collective-permute-start | bytes 786440 | tf_op jit(solution)/shard_map/ppermute | solution.py:291
  35.3 0.2 fusion
  35.5 0.1 fusion.1.back_ref
  35.6 0.0 all-to-all-done.rows_ref
  35.6 0.0 copy-start.2
  35.6 0.6 copy-done.2
  36.2 1.5 %spread_total.3 = f32[16,1,128]{2,1,0:T(1,128)} custom-call(f32[32,1,128]{2,1,0:T(1,128)} %copy-done.2), custom_call_target="tpu_custom_call" | custom-call | tf_op jit(solution)/shard_map/spread_total/pallas_call | solution.py:200
  37.7 0.0 copy-start.1
  37.7 3.6 %kept_grads.1.g_ref = bf16[128,4096]{1,0:T(8,128)(2,1)} custom-call(s32[1,128]{1,0:T(1,128)} %mask_ref, bf16[128,4096]{1,0:T(8,128)(2,1)} %bitcast.14), custom_call_target="tpu_custom_call" | custom-call | tf_op jit(solution)/shard_map/kept_grads/pallas_call | solution.py:188
  41.3 0.0 collective-permute-done.3.far_ref
  41.3 4.4 %collective-permute-done.2.mid_ref = bf16[2,128,512]{2,1,0:T(8,128)(2,1)S(1)} collective-permute-done((bf16[2,128,512]{2,1,0:T(8,128)(2,1)S(1)}, bf16[2,128,512]{2,1,0:T(8,128)(2,1)S(1)}, u32[]{:S(2)}, u32[]{:S(2)}) %collective-permute-start.2) | collective-permute-done | bytes 262176 | tf_op jit(solution)/shard_map/ppermute | solution.py:291
  45.7 0.0 copy-done.1
  45.7 0.0 copy-start
  45.7 1.2 %copy-done = bf16[128,4096]{1,0:T(8,128)(2,1)S(1)} copy-done((bf16[128,4096]{1,0:T(8,128)(2,1)S(1)}, bf16[128,4096]{1,0:T(8,128)(2,1)}, u32[]{:S(2)}) %copy-start) | copy-done | bytes 1048600
  46.9 9.8 %attention.1 = (bf16[128,4096]{1,0:T(8,128)(2,1)}, bf16[128,4096]{1,0:T(8,128)(2,1)S(1)}, f32[2,128,512]{2,1,0:T(8,128)S(1)}, bf16[2,128,512]{2,1,0:T(8,128)(2,1...) custom-call(s32[2]{0:T(128)S(1)} %fusion.1.back_ref, ...), custom_call_target="tpu_custom_call" | custom-call | tf_op jit(solution)/shard_map/attention/pallas_call | solution.py:156
  56.7 2.3 %collective-permute-start.4 = (bf16[2,128,512]{2,1,0:T(8,128)(2,1)S(1)}, bf16[2,128,512]{2,1,0:T(8,128)(2,1)S(1)}, u32[]{:S(2)}, u32[]{:S(2)}) collective-permute-start(bf16[2,128,512]{2,1,0:T(8,128)(2,1)S(1)} %get-tuple-element.21), channel_id=1, source_target_pairs={{0,31},{1,0},{2,1},{3,2},{4,3},{5,4},{6,5},{7,6},{8,7},{9,8},{10,9... | collective-permute-start | bytes 786440 | tf_op jit(solution)/shard_map/ppermute | solution.py:291
  59.0 3.0 %collective-permute-start.5 = (bf16[2,128,512]{2,1,0:T(8,128)(2,1)S(1)}, bf16[2,128,512]{2,1,0:T(8,128)(2,1)S(1)}, u32[]{:S(2)}, u32[]{:S(2)}) collective-permute-start(bf16[2,128,512]{2,1,0:T(8,128)(2,1)S(1)} %get-tuple-element.23), channel_id=1, source_target_pairs={{0,1},{1,2},{2,3},{3,4},{4,5},{5,6},{6,7},{7,8},{8,9},{9,10},{10,1... | collective-permute-start | bytes 786440 | tf_op jit(solution)/shard_map/ppermute | solution.py:291
  62.0 2.8 %collective-permute-done.4 = bf16[2,128,512]{2,1,0:T(8,128)(2,1)S(1)} collective-permute-done((bf16[2,128,512]{2,1,0:T(8,128)(2,1)S(1)}, bf16[2,128,512]{2,1,0:T(8,128)(2,1)S(1)}, u32[]{:S(2)}, u32[]{:S(2)}) %collective-permute-start.4) | collective-permute-done | bytes 262176 | tf_op jit(solution)/shard_map/ppermute | solution.py:291
  64.8 0.1 add.10
  64.9 6.2 %collective-permute-start.6 = (bf16[2,128,512]{2,1,0:T(8,128)(2,1)S(1)}, bf16[2,128,512]{2,1,0:T(8,128)(2,1)S(1)}, u32[]{:S(2)}, u32[]{:S(2)}) collective-permute-start(bf16[2,128,512]{2,1,0:T(8,128)(2,1)S(1)} %add.10), channel_id=1, source_target_pairs={{0,31},{1,0},{2,1},{3,2},{4,3},{5,4},{6,5},{7,6},{8,7},{9,8},{10,9... | collective-permute-start | bytes 786440 | tf_op jit(solution)/shard_map/ppermute | solution.py:291
  71.1 0.0 collective-permute-done.5
  71.1 0.0 copy-start.3
  71.1 0.1 add.11
  71.2 3.0 %collective-permute-start.7 = (bf16[2,128,512]{2,1,0:T(8,128)(2,1)S(1)}, bf16[2,128,512]{2,1,0:T(8,128)(2,1)S(1)}, u32[]{:S(2)}, u32[]{:S(2)}) collective-permute-start(bf16[2,128,512]{2,1,0:T(8,128)(2,1)S(1)} %add.11), channel_id=1, source_target_pairs={{0,28},{1,29},{2,30},{3,31},{4,0},{5,1},{6,2},{7,3},{8,4},{9,5},{1... | collective-permute-start | bytes 786440 | tf_op jit(solution)/shard_map/ppermute | solution.py:291
  74.3 0.0 copy-done.3
  74.3 16.4 %all_to_all.10.rows_ref = f32[16,1,128]{2,1,0:T(1,128)S(1)} all-to-all(f32[16,1,128]{2,1,0:T(1,128)S(1)} %copy-done.3), channel_id=1, replica_groups=mesh['dp'=16,'ctx'=32] {'dp'}, dimensions={0} | all-to-all | bytes 16384 | tf_op jit(solution)/shard_map/all_to_all | solution.py:262
  90.7 0.0 collective-permute-done.6.near_ref
  90.7 0.0 collective-permute-done.7.fourth_ref
  90.7 1.3 %gradients.1 = (bf16[128,4096]{1,0:T(8,128)(2,1)}, bf16[128,512]{1,0:T(8,128)(2,1)}, bf16[128,512]{1,0:T(8,128)(2,1)}) custom-call(f32[16,1,128]{2,1,0:T(1,128)S(1)} %all_to_all.10.rows_ref, bf16[128,4096]{1,0:T(8,128)(2,1)S(1)} %get-tuple-element.25.dq_ref, f32[2,128,512]{2,1,0:T(8,128)S(1)} %get-tuple-element.26.own_ref, ...), custom_call_target="tpu_custom_call" | custom-call | tf_op jit(solution)/shard_map/gradients/pallas_call | solution.py:246
  (1 shorter events, 0.0 us)
Async XLA Ops:
  1.7 23.7 %collective-permute-start.1 = (bf16[2,128,512]{2,1,0:T(8,128)(2,1)S(1)}, bf16[2,128,512]{2,1,0:T(8,128)(2,1)S(1)}, u32[]{:S(2)}, u32[]{:S(2)}) collective-permute-start(bf16[2,128,512]{2,1,0:T(8,128)(2,1)S(1)} %broadcast_select_fusion.own_ref), channel_id=1, source_target_pairs={{0,4},{1,5},{2,6},{3,7},{4,8},{5,9},{6,10},{7,11},{8,12},{9,13},{1... | collective-permute-start | bytes 786440 | tf_op jit(solution)/shard_map/ppermute | solution.py:291
  13.2 20.2 %collective-permute-start = (bf16[2,128,512]{2,1,0:T(8,128)(2,1)S(1)}, bf16[2,128,512]{2,1,0:T(8,128)(2,1)S(1)}, u32[]{:S(2)}, u32[]{:S(2)}) collective-permute-start(bf16[2,128,512]{2,1,0:T(8,128)(2,1)S(1)} %broadcast_select_fusion.own_ref), channel_id=1, source_target_pairs={{0,1},{1,2},{2,3},{3,4},{4,5},{5,6},{6,7},{7,8},{8,9},{9,10},{10,1... | collective-permute-start | bytes 786440 | tf_op jit(solution)/shard_map/ppermute | solution.py:291
  17.7 17.9 %all-to-all-start = ((f32[32,1,128]{2,1,0:T(1,128)}), f32[32,1,128]{2,1,0:T(1,128)S(1)}, u32[]{:S(2)}, u32[]{:S(2)}) async-start(f32[32,1,128]{2,1,0:T(1,128)} %spread_total.2), calls=%async_computation | async-start | bytes 32768 | tf_op jit(solution)/shard_map/all_to_all | solution.py:262
  23.9 0.7 copy-start.4
  24.7 0.7 copy-start.5
  25.4 15.9 %collective-permute-start.3 = (bf16[2,128,512]{2,1,0:T(8,128)(2,1)S(1)}, bf16[2,128,512]{2,1,0:T(8,128)(2,1)S(1)}, u32[]{:S(2)}, u32[]{:S(2)}) collective-permute-start(bf16[2,128,512]{2,1,0:T(8,128)(2,1)S(1)} %collective-permute-done.1.fourth_ref), channel_id=1, source_target_pairs={{0,31},{1,0},{2,1},{3,2},{4,3},{5,4},{6,5},{7,6},{8,7},{9,8},{10,9... | collective-permute-start | bytes 786440 | tf_op jit(solution)/shard_map/ppermute | solution.py:291
  33.4 12.3 %collective-permute-start.2 = (bf16[2,128,512]{2,1,0:T(8,128)(2,1)S(1)}, bf16[2,128,512]{2,1,0:T(8,128)(2,1)S(1)}, u32[]{:S(2)}, u32[]{:S(2)}) collective-permute-start(bf16[2,128,512]{2,1,0:T(8,128)(2,1)S(1)} %collective-permute-done.near_ref), channel_id=1, source_target_pairs={{0,1},{1,2},{2,3},{3,4},{4,5},{5,6},{6,7},{7,8},{8,9},{9,10},{10,1... | collective-permute-start | bytes 786440 | tf_op jit(solution)/shard_map/ppermute | solution.py:291
  35.6 0.6 copy-start.2
  37.7 8.0 %copy-start.1 = (bf16[1,128,4096]{2,1,0:T(8,128)(2,1)S(1)}, bf16[1,128,4096]{2,1,0:T(8,128)(2,1)}, u32[]{:S(2)}) copy-start(bf16[1,128,4096]{2,1,0:T(8,128)(2,1)} %param.7) | copy-start | bytes 3145732
  45.7 1.2 %copy-start = (bf16[128,4096]{1,0:T(8,128)(2,1)S(1)}, bf16[128,4096]{1,0:T(8,128)(2,1)}, u32[]{:S(2)}) copy-start(bf16[128,4096]{1,0:T(8,128)(2,1)} %kept_grads.1.g_ref) | copy-start | bytes 3145732
  56.7 8.1 %collective-permute-start.4 = (bf16[2,128,512]{2,1,0:T(8,128)(2,1)S(1)}, bf16[2,128,512]{2,1,0:T(8,128)(2,1)S(1)}, u32[]{:S(2)}, u32[]{:S(2)}) collective-permute-start(bf16[2,128,512]{2,1,0:T(8,128)(2,1)S(1)} %get-tuple-element.21), channel_id=1, source_target_pairs={{0,31},{1,0},{2,1},{3,2},{4,3},{5,4},{6,5},{7,6},{8,7},{9,8},{10,9... | collective-permute-start | bytes 786440 | tf_op jit(solution)/shard_map/ppermute | solution.py:291
  59.0 12.1 %collective-permute-start.5 = (bf16[2,128,512]{2,1,0:T(8,128)(2,1)S(1)}, bf16[2,128,512]{2,1,0:T(8,128)(2,1)S(1)}, u32[]{:S(2)}, u32[]{:S(2)}) collective-permute-start(bf16[2,128,512]{2,1,0:T(8,128)(2,1)S(1)} %get-tuple-element.23), channel_id=1, source_target_pairs={{0,1},{1,2},{2,3},{3,4},{4,5},{5,6},{6,7},{7,8},{8,9},{9,10},{10,1... | collective-permute-start | bytes 786440 | tf_op jit(solution)/shard_map/ppermute | solution.py:291
  64.9 25.8 %collective-permute-start.6 = (bf16[2,128,512]{2,1,0:T(8,128)(2,1)S(1)}, bf16[2,128,512]{2,1,0:T(8,128)(2,1)S(1)}, u32[]{:S(2)}, u32[]{:S(2)}) collective-permute-start(bf16[2,128,512]{2,1,0:T(8,128)(2,1)S(1)} %add.10), channel_id=1, source_target_pairs={{0,31},{1,0},{2,1},{3,2},{4,3},{5,4},{6,5},{7,6},{8,7},{9,8},{10,9... | collective-permute-start | bytes 786440 | tf_op jit(solution)/shard_map/ppermute | solution.py:291
  71.1 3.1 %copy-start.3 = (f32[16,1,128]{2,1,0:T(1,128)S(1)}, f32[16,1,128]{2,1,0:T(1,128)}, u32[]{:S(2)}) copy-start(f32[16,1,128]{2,1,0:T(1,128)} %spread_total.3) | copy-start | bytes 24580
  71.2 19.5 %collective-permute-start.7 = (bf16[2,128,512]{2,1,0:T(8,128)(2,1)S(1)}, bf16[2,128,512]{2,1,0:T(8,128)(2,1)S(1)}, u32[]{:S(2)}, u32[]{:S(2)}) collective-permute-start(bf16[2,128,512]{2,1,0:T(8,128)(2,1)S(1)} %add.11), channel_id=1, source_target_pairs={{0,28},{1,29},{2,30},{3,31},{4,0},{5,1},{6,2},{7,3},{8,4},{9,5},{1... | collective-permute-start | bytes 786440 | tf_op jit(solution)/shard_map/ppermute | solution.py:291

commit v4 on v3

--- a/solution.py
+++ b/solution.py
@@ -184,13 +184,10 @@
 
 
 def kept_grads(mask, grads):
-    columns = pl.BlockSpec((grads.shape[0], GROUP * HEAD_WIDTH), lambda i: (0, i))
     return pl.pallas_call(
         kept_kernel,
-        grid=(KEY_VALUE_HEADS,),
-        in_specs=[pl.BlockSpec(mask.shape, lambda i: (0, 0)), columns],
-        out_specs=columns,
-        out_shape=jax.ShapeDtypeStruct(grads.shape, grads.dtype),
+        out_specs=pl.BlockSpec(memory_space=pltpu.VMEM),
+        out_shape=pltpu.VMEM(grads.shape, grads.dtype),
         cost_estimate=pl.CostEstimate(flops=0, bytes_accessed=0, transcendentals=0),
         name="kept_grads",
     )(mask, grads)

time: 92.6 us -> 91.2 us (0.985)
  waiting for transfers between devices: 8.59 us -> 10.6 us
  Pallas kernels: 17.6 us -> 15.6 us
  local copies, waits for them, and re-layouts: 3.22 us -> 1.99 us
    pallas_call x1, Pallas kernels: 3.63 us -> 1.57 us  [kept_grads(): pl.pallas_call(kept_kernel, out_specs=pl.BlockSpec(memory_space=pltpu.VME...]
    ppermute x8, waiting for transfers between devices: 8.59 us -> 10.6 us  [shift(): return lax.ppermute(array, 'ctx', pairs)]
    unnamed x12 -> x10, local copies, waits for them, and re-layouts: 3.15 us -> 1.92 us
  transfers between devices with their start and end apart: 9 -> 9, of which waited for: 3 -> 3; matrix products, arithmetic and copies ran while one was open for 1% -> 1% of each run, Pallas kernels for 7% -> 5%
where the time goes in v4:
time: 91.2 us; the launch traced here: 90.6 us
  starting transfers between devices  43.5 us (48%)
  blocking collectives  16.5 us (18%)
  Pallas kernels  15.6 us (17%)
  waiting for transfers between devices  10.6 us (12%)
  local copies, waits for them, and re-layouts  1.99 us (2%)
  other arithmetic  1.57 us (2%)
    ppermute x8, starting transfers between devices, shift(): return lax.ppermute(array, 'ctx', pairs)  37.3 us
    all_to_all x1, blocking collectives, exchanged(): return lax.all_to_all(rows, axis, split_axis=0, concat_axis=0)  16.5 us
    ppermute x8, waiting for transfers between devices, shift(): return lax.ppermute(array, 'ctx', pairs)  10.6 us
    pallas_call x1, Pallas kernels, attention(): pl.pallas_call(attention_kernel, in_specs=[pl.BlockSpec(memory_space=pltp...  9.88 us
    all_to_all x1, starting transfers between devices, exchanged(): return lax.all_to_all(rows, axis, split_axis=0, concat_axis=0)  6.24 us
    pallas_call x2, Pallas kernels, spread_total(): pl.pallas_call(total_kernel, in_specs=[pl.BlockSpec(memory_space=space)],...  2.86 us
    unnamed x10, local copies, waits for them, and re-layouts  1.92 us
  transfers between devices with their start and end apart: 9, of which 3 were waited for; matrix products, arithmetic and copies ran while one was open for 1% of the time, Pallas kernels for 5%

profile of v4, /device:TPU:1, one launch (start us, length us, event | category | flops | bytes accessed | tf_op | source)
XLA Modules:
  0.0 90.6 jit_solution(9767941862580306467)
XLA Ops:
  0.6 1.1 %broadcast_select_fusion.own_ref = bf16[2,128,512]{2,1,0:T(8,128)(2,1)S(1)} fusion(pred[2]{0:T(512)(128)(4,1)S(1)} %iota_compare_fusion.1, bf16[128,512]{1,0:T(8,128)(2,1)} %bitcast.15, bf16[128,512]{1,0:T(8,128)(2,1)} %bitcast.16), kind=kLoop, calls=%fused_computation | loop fusion | flops 131072 | bytes 524290 | tf_op jit(solution)/shard_map/jit(_where)/select_n | solution.py:291
  1.7 11.5 %collective-permute-start.1 = (bf16[2,128,512]{2,1,0:T(8,128)(2,1)S(1)}, bf16[2,128,512]{2,1,0:T(8,128)(2,1)S(1)}, u32[]{:S(2)}, u32[]{:S(2)}) collective-permute-start(bf16[2,128,512]{2,1,0:T(8,128)(2,1)S(1)} %broadcast_select_fusion.own_ref), channel_id=1, source_target_pairs={{0,4},{1,5},{2,6},{3,7},{4,8},{5,9},{6,10},{7,11},{8,12},{9,13},{1... | collective-permute-start | bytes 786440 | tf_op jit(solution)/shard_map/ppermute | solution.py:288
  13.2 3.1 %collective-permute-start = (bf16[2,128,512]{2,1,0:T(8,128)(2,1)S(1)}, bf16[2,128,512]{2,1,0:T(8,128)(2,1)S(1)}, u32[]{:S(2)}, u32[]{:S(2)}) collective-permute-start(bf16[2,128,512]{2,1,0:T(8,128)(2,1)S(1)} %broadcast_select_fusion.own_ref), channel_id=1, source_target_pairs={{0,1},{1,2},{2,3},{3,4},{4,5},{5,6},{6,7},{7,8},{8,9},{9,10},{10,1... | collective-permute-start | bytes 786440 | tf_op jit(solution)/shard_map/ppermute | solution.py:288
  16.3 1.4 %spread_total.2 = f32[32,1,128]{2,1,0:T(1,128)} custom-call(s32[1,128]{1,0:T(1,128)} %mask_ref), custom_call_target="tpu_custom_call" | custom-call | tf_op jit(solution)/shard_map/spread_total/pallas_call | solution.py:197
  17.7 6.2 %all-to-all-start = ((f32[32,1,128]{2,1,0:T(1,128)}), f32[32,1,128]{2,1,0:T(1,128)S(1)}, u32[]{:S(2)}, u32[]{:S(2)}) async-start(f32[32,1,128]{2,1,0:T(1,128)} %spread_total.2), calls=%async_computation | async-start | bytes 32768 | tf_op jit(solution)/shard_map/all_to_all | solution.py:259
  23.9 0.0 copy-start.3
  23.9 0.6 copy-done.3
  24.6 0.1 dynamic-slice_bitcast_fusion
  24.7 0.0 copy-start.4
  24.7 0.7 copy-done.4
  25.3 0.1 select_reduce_fusion
  25.4 0.0 collective-permute-done.1.fourth_ref
  25.4 6.6 %collective-permute-start.3 = (bf16[2,128,512]{2,1,0:T(8,128)(2,1)S(1)}, bf16[2,128,512]{2,1,0:T(8,128)(2,1)S(1)}, u32[]{:S(2)}, u32[]{:S(2)}) collective-permute-start(bf16[2,128,512]{2,1,0:T(8,128)(2,1)S(1)} %collective-permute-done.1.fourth_ref), channel_id=1, source_target_pairs={{0,31},{1,0},{2,1},{3,2},{4,3},{5,4},{6,5},{7,6},{8,7},{9,8},{10,9... | collective-permute-start | bytes 786440 | tf_op jit(solution)/shard_map/ppermute | solution.py:288
  32.0 1.4 %collective-permute-done.near_ref = bf16[2,128,512]{2,1,0:T(8,128)(2,1)S(1)} collective-permute-done((bf16[2,128,512]{2,1,0:T(8,128)(2,1)S(1)}, bf16[2,128,512]{2,1,0:T(8,128)(2,1)S(1)}, u32[]{:S(2)}, u32[]{:S(2)}) %collective-permute-start) | collective-permute-done | bytes 262176 | tf_op jit(solution)/shard_map/ppermute | solution.py:288
  33.4 1.9 %collective-permute-start.2 = (bf16[2,128,512]{2,1,0:T(8,128)(2,1)S(1)}, bf16[2,128,512]{2,1,0:T(8,128)(2,1)S(1)}, u32[]{:S(2)}, u32[]{:S(2)}) collective-permute-start(bf16[2,128,512]{2,1,0:T(8,128)(2,1)S(1)} %collective-permute-done.near_ref), channel_id=1, source_target_pairs={{0,1},{1,2},{2,3},{3,4},{4,5},{5,6},{6,7},{7,8},{8,9},{9,10},{10,1... | collective-permute-start | bytes 786440 | tf_op jit(solution)/shard_map/ppermute | solution.py:288
  35.3 0.2 fusion
  35.5 0.1 fusion.1.back_ref
  35.6 0.0 all-to-all-done.rows_ref
  35.6 0.0 copy-start.1
  35.6 0.6 copy-done.1
  36.2 1.5 %spread_total.3 = f32[16,1,128]{2,1,0:T(1,128)} custom-call(f32[32,1,128]{2,1,0:T(1,128)} %copy-done.1), custom_call_target="tpu_custom_call" | custom-call | tf_op jit(solution)/shard_map/spread_total/pallas_call | solution.py:197
  37.7 0.0 copy-start
  37.7 1.6 %kept_grads.1.g_ref = bf16[128,4096]{1,0:T(8,128)(2,1)S(1)} custom-call(s32[1,128]{1,0:T(1,128)} %mask_ref, bf16[128,4096]{1,0:T(8,128)(2,1)} %bitcast.14), custom_call_target="tpu_custom_call" | custom-call | tf_op jit(solution)/shard_map/kept_grads/pallas_call | solution.py:187
  39.2 0.0 collective-permute-done.3.far_ref
  39.3 6.4 %collective-permute-done.2.mid_ref = bf16[2,128,512]{2,1,0:T(8,128)(2,1)S(1)} collective-permute-done((bf16[2,128,512]{2,1,0:T(8,128)(2,1)S(1)}, bf16[2,128,512]{2,1,0:T(8,128)(2,1)S(1)}, u32[]{:S(2)}, u32[]{:S(2)}) %collective-permute-start.2) | collective-permute-done | bytes 262176 | tf_op jit(solution)/shard_map/ppermute | solution.py:288
  45.7 0.0 copy-done
  45.7 9.9 %attention.1 = (bf16[128,4096]{1,0:T(8,128)(2,1)}, bf16[128,4096]{1,0:T(8,128)(2,1)S(1)}, f32[2,128,512]{2,1,0:T(8,128)S(1)}, bf16[2,128,512]{2,1,0:T(8,128)(2,1...) custom-call(s32[2]{0:T(128)S(1)} %fusion.1.back_ref, ...), custom_call_target="tpu_custom_call" | custom-call | tf_op jit(solution)/shard_map/attention/pallas_call | solution.py:156
  55.6 1.9 %collective-permute-start.4 = (bf16[2,128,512]{2,1,0:T(8,128)(2,1)S(1)}, bf16[2,128,512]{2,1,0:T(8,128)(2,1)S(1)}, u32[]{:S(2)}, u32[]{:S(2)}) collective-permute-start(bf16[2,128,512]{2,1,0:T(8,128)(2,1)S(1)} %get-tuple-element.21), channel_id=1, source_target_pairs={{0,31},{1,0},{2,1},{3,2},{4,3},{5,4},{6,5},{7,6},{8,7},{9,8},{10,9... | collective-permute-start | bytes 786440 | tf_op jit(solution)/shard_map/ppermute | solution.py:288
  57.5 3.4 %collective-permute-start.5 = (bf16[2,128,512]{2,1,0:T(8,128)(2,1)S(1)}, bf16[2,128,512]{2,1,0:T(8,128)(2,1)S(1)}, u32[]{:S(2)}, u32[]{:S(2)}) collective-permute-start(bf16[2,128,512]{2,1,0:T(8,128)(2,1)S(1)} %get-tuple-element.23), channel_id=1, source_target_pairs={{0,1},{1,2},{2,3},{3,4},{4,5},{5,6},{6,7},{7,8},{8,9},{9,10},{10,1... | collective-permute-start | bytes 786440 | tf_op jit(solution)/shard_map/ppermute | solution.py:288
  60.9 2.8 %collective-permute-done.4 = bf16[2,128,512]{2,1,0:T(8,128)(2,1)S(1)} collective-permute-done((bf16[2,128,512]{2,1,0:T(8,128)(2,1)S(1)}, bf16[2,128,512]{2,1,0:T(8,128)(2,1)S(1)}, u32[]{:S(2)}, u32[]{:S(2)}) %collective-permute-start.4) | collective-permute-done | bytes 262176 | tf_op jit(solution)/shard_map/ppermute | solution.py:288
  63.6 0.1 add.10
  63.7 5.5 %collective-permute-start.6 = (bf16[2,128,512]{2,1,0:T(8,128)(2,1)S(1)}, bf16[2,128,512]{2,1,0:T(8,128)(2,1)S(1)}, u32[]{:S(2)}, u32[]{:S(2)}) collective-permute-start(bf16[2,128,512]{2,1,0:T(8,128)(2,1)S(1)} %add.10), channel_id=1, source_target_pairs={{0,31},{1,0},{2,1},{3,2},{4,3},{5,4},{6,5},{7,6},{8,7},{9,8},{10,9... | collective-permute-start | bytes 786440 | tf_op jit(solution)/shard_map/ppermute | solution.py:288
  69.2 0.0 collective-permute-done.5
  69.2 0.0 copy-start.2
  69.3 0.1 add.11
  69.3 3.4 %collective-permute-start.7 = (bf16[2,128,512]{2,1,0:T(8,128)(2,1)S(1)}, bf16[2,128,512]{2,1,0:T(8,128)(2,1)S(1)}, u32[]{:S(2)}, u32[]{:S(2)}) collective-permute-start(bf16[2,128,512]{2,1,0:T(8,128)(2,1)S(1)} %add.11), channel_id=1, source_target_pairs={{0,28},{1,29},{2,30},{3,31},{4,0},{5,1},{6,2},{7,3},{8,4},{9,5},{1... | collective-permute-start | bytes 786440 | tf_op jit(solution)/shard_map/ppermute | solution.py:288
  72.8 0.0 copy-done.2
  72.8 16.5 %all_to_all.10.rows_ref = f32[16,1,128]{2,1,0:T(1,128)S(1)} all-to-all(f32[16,1,128]{2,1,0:T(1,128)S(1)} %copy-done.2), channel_id=1, replica_groups=mesh['dp'=16,'ctx'=32] {'dp'}, dimensions={0} | all-to-all | bytes 16384 | tf_op jit(solution)/shard_map/all_to_all | solution.py:259
  89.3 0.0 collective-permute-done.6.near_ref
  89.3 0.0 collective-permute-done.7.fourth_ref
  89.3 1.3 %gradients.1 = (bf16[128,4096]{1,0:T(8,128)(2,1)}, bf16[128,512]{1,0:T(8,128)(2,1)}, bf16[128,512]{1,0:T(8,128)(2,1)}) custom-call(f32[16,1,128]{2,1,0:T(1,128)S(1)} %all_to_all.10.rows_ref, bf16[128,4096]{1,0:T(8,128)(2,1)S(1)} %get-tuple-element.25.dq_ref, f32[2,128,512]{2,1,0:T(8,128)S(1)} %get-tuple-element.26.own_ref, ...), custom_call_target="tpu_custom_call" | custom-call | tf_op jit(solution)/shard_map/gradients/pallas_call | solution.py:243
  (1 shorter events, 0.0 us)
Async XLA Ops:
  1.7 23.7 %collective-permute-start.1 = (bf16[2,128,512]{2,1,0:T(8,128)(2,1)S(1)}, bf16[2,128,512]{2,1,0:T(8,128)(2,1)S(1)}, u32[]{:S(2)}, u32[]{:S(2)}) collective-permute-start(bf16[2,128,512]{2,1,0:T(8,128)(2,1)S(1)} %broadcast_select_fusion.own_ref), channel_id=1, source_target_pairs={{0,4},{1,5},{2,6},{3,7},{4,8},{5,9},{6,10},{7,11},{8,12},{9,13},{1... | collective-permute-start | bytes 786440 | tf_op jit(solution)/shard_map/ppermute | solution.py:288
  13.2 20.2 %collective-permute-start = (bf16[2,128,512]{2,1,0:T(8,128)(2,1)S(1)}, bf16[2,128,512]{2,1,0:T(8,128)(2,1)S(1)}, u32[]{:S(2)}, u32[]{:S(2)}) collective-permute-start(bf16[2,128,512]{2,1,0:T(8,128)(2,1)S(1)} %broadcast_select_fusion.own_ref), channel_id=1, source_target_pairs={{0,1},{1,2},{2,3},{3,4},{4,5},{5,6},{6,7},{7,8},{8,9},{9,10},{10,1... | collective-permute-start | bytes 786440 | tf_op jit(solution)/shard_map/ppermute | solution.py:288
  17.7 17.9 %all-to-all-start = ((f32[32,1,128]{2,1,0:T(1,128)}), f32[32,1,128]{2,1,0:T(1,128)S(1)}, u32[]{:S(2)}, u32[]{:S(2)}) async-start(f32[32,1,128]{2,1,0:T(1,128)} %spread_total.2), calls=%async_computation | async-start | bytes 32768 | tf_op jit(solution)/shard_map/all_to_all | solution.py:259
  23.9 0.7 copy-start.3
  24.7 0.7 copy-start.4
  25.4 13.8 %collective-permute-start.3 = (bf16[2,128,512]{2,1,0:T(8,128)(2,1)S(1)}, bf16[2,128,512]{2,1,0:T(8,128)(2,1)S(1)}, u32[]{:S(2)}, u32[]{:S(2)}) collective-permute-start(bf16[2,128,512]{2,1,0:T(8,128)(2,1)S(1)} %collective-permute-done.1.fourth_ref), channel_id=1, source_target_pairs={{0,31},{1,0},{2,1},{3,2},{4,3},{5,4},{6,5},{7,6},{8,7},{9,8},{10,9... | collective-permute-start | bytes 786440 | tf_op jit(solution)/shard_map/ppermute | solution.py:288
  33.4 12.3 %collective-permute-start.2 = (bf16[2,128,512]{2,1,0:T(8,128)(2,1)S(1)}, bf16[2,128,512]{2,1,0:T(8,128)(2,1)S(1)}, u32[]{:S(2)}, u32[]{:S(2)}) collective-permute-start(bf16[2,128,512]{2,1,0:T(8,128)(2,1)S(1)} %collective-permute-done.near_ref), channel_id=1, source_target_pairs={{0,1},{1,2},{2,3},{3,4},{4,5},{5,6},{6,7},{7,8},{8,9},{9,10},{10,1... | collective-permute-start | bytes 786440 | tf_op jit(solution)/shard_map/ppermute | solution.py:288
  35.6 0.6 copy-start.1
  37.7 8.0 %copy-start = (bf16[1,128,4096]{2,1,0:T(8,128)(2,1)S(1)}, bf16[1,128,4096]{2,1,0:T(8,128)(2,1)}, u32[]{:S(2)}) copy-start(bf16[1,128,4096]{2,1,0:T(8,128)(2,1)} %param.7) | copy-start | bytes 3145732
  55.6 8.1 %collective-permute-start.4 = (bf16[2,128,512]{2,1,0:T(8,128)(2,1)S(1)}, bf16[2,128,512]{2,1,0:T(8,128)(2,1)S(1)}, u32[]{:S(2)}, u32[]{:S(2)}) collective-permute-start(bf16[2,128,512]{2,1,0:T(8,128)(2,1)S(1)} %get-tuple-element.21), channel_id=1, source_target_pairs={{0,31},{1,0},{2,1},{3,2},{4,3},{5,4},{6,5},{7,6},{8,7},{9,8},{10,9... | collective-permute-start | bytes 786440 | tf_op jit(solution)/shard_map/ppermute | solution.py:288
  57.5 11.7 %collective-permute-start.5 = (bf16[2,128,512]{2,1,0:T(8,128)(2,1)S(1)}, bf16[2,128,512]{2,1,0:T(8,128)(2,1)S(1)}, u32[]{:S(2)}, u32[]{:S(2)}) collective-permute-start(bf16[2,128,512]{2,1,0:T(8,128)(2,1)S(1)} %get-tuple-element.23), channel_id=1, source_target_pairs={{0,1},{1,2},{2,3},{3,4},{4,5},{5,6},{6,7},{7,8},{8,9},{9,10},{10,1... | collective-permute-start | bytes 786440 | tf_op jit(solution)/shard_map/ppermute | solution.py:288
  63.7 25.6 %collective-permute-start.6 = (bf16[2,128,512]{2,1,0:T(8,128)(2,1)S(1)}, bf16[2,128,512]{2,1,0:T(8,128)(2,1)S(1)}, u32[]{:S(2)}, u32[]{:S(2)}) collective-permute-start(bf16[2,128,512]{2,1,0:T(8,128)(2,1)S(1)} %add.10), channel_id=1, source_target_pairs={{0,31},{1,0},{2,1},{3,2},{4,3},{5,4},{6,5},{7,6},{8,7},{9,8},{10,9... | collective-permute-start | bytes 786440 | tf_op jit(solution)/shard_map/ppermute | solution.py:288
  69.2 3.5 %copy-start.2 = (f32[16,1,128]{2,1,0:T(1,128)S(1)}, f32[16,1,128]{2,1,0:T(1,128)}, u32[]{:S(2)}) copy-start(f32[16,1,128]{2,1,0:T(1,128)} %spread_total.3) | copy-start | bytes 24580
  69.3 20.0 %collective-permute-start.7 = (bf16[2,128,512]{2,1,0:T(8,128)(2,1)S(1)}, bf16[2,128,512]{2,1,0:T(8,128)(2,1)S(1)}, u32[]{:S(2)}, u32[]{:S(2)}) collective-permute-start(bf16[2,128,512]{2,1,0:T(8,128)(2,1)S(1)} %add.11), channel_id=1, source_target_pairs={{0,28},{1,29},{2,30},{3,31},{4,0},{5,1},{6,2},{7,3},{8,4},{9,5},{1... | collective-permute-start | bytes 786440 | tf_op jit(solution)/shard_map/ppermute | solution.py:288

commit v5 on v4

--- a/solution.py
+++ b/solution.py
@@ -127,13 +127,16 @@
         now = ahead
         if n + 1 < len(steps):
             ahead = products(*steps[n + 1], *sides[steps[n + 1][0]])
-        if t == 0:
-            keys_acc[...] = jnp.zeros_like(keys_acc)
-            values_acc[...] = jnp.zeros_like(values_acc)
         keys, values = sides[k]
         p_low, ds = probabilities(t, *now)
-        keys_acc[window(t), :] += dot_nn(ds, query_rows(k, t))
-        values_acc[window(t), :] += dot_nn(p_low, grad_rows(k, t))
+        terms = dot_nn(ds, query_rows(k, t)), dot_nn(p_low, grad_rows(k, t))
+        for acc, term in zip((keys_acc, values_acc), terms):
+            if t == 0:
+                for rest in (slice(0, window(0).start), slice(window(0).stop, rows)):
+                    acc[rest, :] = jnp.zeros((rest.stop - rest.start, width), jnp.float32)
+                acc[window(0), :] = term
+            else:
+                acc[window(t), :] += term
         out = dot_tn(p_low, values[window(t)]).astype(jnp.bfloat16)
         dq = (dot_tn(ds, keys[window(t)]) * SCALE).astype(jnp.bfloat16)
         place = (slice(t * block, (t + 1) * block), slice(k * group, (k + 1) * group))

time: 91.2 us -> 91 us (level)
  no operation moved by 1% of the time
where the time goes in v5:
time: 91 us; the launch traced here: 90.5 us
  starting transfers between devices  43.5 us (48%)
  blocking collectives  16.5 us (18%)
  Pallas kernels  15.5 us (17%)
  waiting for transfers between devices  10.6 us (12%)
  local copies, waits for them, and re-layouts  1.99 us (2%)
  other arithmetic  1.57 us (2%)
    ppermute x8, starting transfers between devices, shift(): return lax.ppermute(array, 'ctx', pairs)  37.2 us
    all_to_all x1, blocking collectives, exchanged(): return lax.all_to_all(rows, axis, split_axis=0, concat_axis=0)  16.5 us
    ppermute x8, waiting for transfers between devices, shift(): return lax.ppermute(array, 'ctx', pairs)  10.6 us
    pallas_call x1, Pallas kernels, attention(): pl.pallas_call(attention_kernel, in_specs=[pl.BlockSpec(memory_space=pltp...  9.72 us
    all_to_all x1, starting transfers between devices, exchanged(): return lax.all_to_all(rows, axis, split_axis=0, concat_axis=0)  6.24 us
    pallas_call x2, Pallas kernels, spread_total(): pl.pallas_call(total_kernel, in_specs=[pl.BlockSpec(memory_space=space)],...  2.86 us
    unnamed x10, local copies, waits for them, and re-layouts  1.92 us
  transfers between devices with their start and end apart: 9, of which 3 were waited for; matrix products, arithmetic and copies ran while one was open for 1% of the time, Pallas kernels for 5%

profile of v5, /device:TPU:1, one launch (start us, length us, event | category | flops | bytes accessed | tf_op | source)
XLA Modules:
  0.0 90.5 jit_solution(10239071049755339129)
XLA Ops:
  0.6 1.1 %broadcast_select_fusion.own_ref = bf16[2,128,512]{2,1,0:T(8,128)(2,1)S(1)} fusion(pred[2]{0:T(512)(128)(4,1)S(1)} %iota_compare_fusion.1, bf16[128,512]{1,0:T(8,128)(2,1)} %bitcast.15, bf16[128,512]{1,0:T(8,128)(2,1)} %bitcast.16), kind=kLoop, calls=%fused_computation | loop fusion | flops 131072 | bytes 524290 | tf_op jit(solution)/shard_map/jit(_where)/select_n | solution.py:294
  1.7 11.5 %collective-permute-start.1 = (bf16[2,128,512]{2,1,0:T(8,128)(2,1)S(1)}, bf16[2,128,512]{2,1,0:T(8,128)(2,1)S(1)}, u32[]{:S(2)}, u32[]{:S(2)}) collective-permute-start(bf16[2,128,512]{2,1,0:T(8,128)(2,1)S(1)} %broadcast_select_fusion.own_ref), channel_id=1, source_target_pairs={{0,4},{1,5},{2,6},{3,7},{4,8},{5,9},{6,10},{7,11},{8,12},{9,13},{1... | collective-permute-start | bytes 786440 | tf_op jit(solution)/shard_map/ppermute | solution.py:291
  13.2 3.1 %collective-permute-start = (bf16[2,128,512]{2,1,0:T(8,128)(2,1)S(1)}, bf16[2,128,512]{2,1,0:T(8,128)(2,1)S(1)}, u32[]{:S(2)}, u32[]{:S(2)}) collective-permute-start(bf16[2,128,512]{2,1,0:T(8,128)(2,1)S(1)} %broadcast_select_fusion.own_ref), channel_id=1, source_target_pairs={{0,1},{1,2},{2,3},{3,4},{4,5},{5,6},{6,7},{7,8},{8,9},{9,10},{10,1... | collective-permute-start | bytes 786440 | tf_op jit(solution)/shard_map/ppermute | solution.py:291
  16.3 1.4 %spread_total.2 = f32[32,1,128]{2,1,0:T(1,128)} custom-call(s32[1,128]{1,0:T(1,128)} %mask_ref), custom_call_target="tpu_custom_call" | custom-call | tf_op jit(solution)/shard_map/spread_total/pallas_call | solution.py:200
  17.7 6.2 %all-to-all-start = ((f32[32,1,128]{2,1,0:T(1,128)}), f32[32,1,128]{2,1,0:T(1,128)S(1)}, u32[]{:S(2)}, u32[]{:S(2)}) async-start(f32[32,1,128]{2,1,0:T(1,128)} %spread_total.2), calls=%async_computation | async-start | bytes 32768 | tf_op jit(solution)/shard_map/all_to_all | solution.py:262
  23.9 0.0 copy-start.3
  23.9 0.6 copy-done.3
  24.6 0.1 dynamic-slice_bitcast_fusion
  24.7 0.0 copy-start.4
  24.7 0.7 copy-done.4
  25.3 0.1 select_reduce_fusion
  25.4 0.0 collective-permute-done.1.fourth_ref
  25.4 6.6 %collective-permute-start.3 = (bf16[2,128,512]{2,1,0:T(8,128)(2,1)S(1)}, bf16[2,128,512]{2,1,0:T(8,128)(2,1)S(1)}, u32[]{:S(2)}, u32[]{:S(2)}) collective-permute-start(bf16[2,128,512]{2,1,0:T(8,128)(2,1)S(1)} %collective-permute-done.1.fourth_ref), channel_id=1, source_target_pairs={{0,31},{1,0},{2,1},{3,2},{4,3},{5,4},{6,5},{7,6},{8,7},{9,8},{10,9... | collective-permute-start | bytes 786440 | tf_op jit(solution)/shard_map/ppermute | solution.py:291
  32.0 1.4 %collective-permute-done.near_ref = bf16[2,128,512]{2,1,0:T(8,128)(2,1)S(1)} collective-permute-done((bf16[2,128,512]{2,1,0:T(8,128)(2,1)S(1)}, bf16[2,128,512]{2,1,0:T(8,128)(2,1)S(1)}, u32[]{:S(2)}, u32[]{:S(2)}) %collective-permute-start) | collective-permute-done | bytes 262176 | tf_op jit(solution)/shard_map/ppermute | solution.py:291
  33.4 1.9 %collective-permute-start.2 = (bf16[2,128,512]{2,1,0:T(8,128)(2,1)S(1)}, bf16[2,128,512]{2,1,0:T(8,128)(2,1)S(1)}, u32[]{:S(2)}, u32[]{:S(2)}) collective-permute-start(bf16[2,128,512]{2,1,0:T(8,128)(2,1)S(1)} %collective-permute-done.near_ref), channel_id=1, source_target_pairs={{0,1},{1,2},{2,3},{3,4},{4,5},{5,6},{6,7},{7,8},{8,9},{9,10},{10,1... | collective-permute-start | bytes 786440 | tf_op jit(solution)/shard_map/ppermute | solution.py:291
  35.3 0.2 fusion
  35.5 0.1 fusion.1.back_ref
  35.6 0.0 all-to-all-done.rows_ref
  35.6 0.0 copy-start.1
  35.6 0.6 copy-done.1
  36.2 1.5 %spread_total.3 = f32[16,1,128]{2,1,0:T(1,128)} custom-call(f32[32,1,128]{2,1,0:T(1,128)} %copy-done.1), custom_call_target="tpu_custom_call" | custom-call | tf_op jit(solution)/shard_map/spread_total/pallas_call | solution.py:200
  37.7 0.0 copy-start
  37.7 1.6 %kept_grads.1.g_ref = bf16[128,4096]{1,0:T(8,128)(2,1)S(1)} custom-call(s32[1,128]{1,0:T(1,128)} %mask_ref, bf16[128,4096]{1,0:T(8,128)(2,1)} %bitcast.14), custom_call_target="tpu_custom_call" | custom-call | tf_op jit(solution)/shard_map/kept_grads/pallas_call | solution.py:190
  39.2 0.0 collective-permute-done.3.far_ref
  39.3 6.4 %collective-permute-done.2.mid_ref = bf16[2,128,512]{2,1,0:T(8,128)(2,1)S(1)} collective-permute-done((bf16[2,128,512]{2,1,0:T(8,128)(2,1)S(1)}, bf16[2,128,512]{2,1,0:T(8,128)(2,1)S(1)}, u32[]{:S(2)}, u32[]{:S(2)}) %collective-permute-start.2) | collective-permute-done | bytes 262176 | tf_op jit(solution)/shard_map/ppermute | solution.py:291
  45.7 0.0 copy-done
  45.7 9.7 %attention.1 = (bf16[128,4096]{1,0:T(8,128)(2,1)}, bf16[128,4096]{1,0:T(8,128)(2,1)S(1)}, f32[2,128,512]{2,1,0:T(8,128)S(1)}, bf16[2,128,512]{2,1,0:T(8,128)(2,1...) custom-call(s32[2]{0:T(128)S(1)} %fusion.1.back_ref, ...), custom_call_target="tpu_custom_call" | custom-call | tf_op jit(solution)/shard_map/attention/pallas_call | solution.py:159
  55.4 1.9 %collective-permute-start.4 = (bf16[2,128,512]{2,1,0:T(8,128)(2,1)S(1)}, bf16[2,128,512]{2,1,0:T(8,128)(2,1)S(1)}, u32[]{:S(2)}, u32[]{:S(2)}) collective-permute-start(bf16[2,128,512]{2,1,0:T(8,128)(2,1)S(1)} %get-tuple-element.21), channel_id=1, source_target_pairs={{0,31},{1,0},{2,1},{3,2},{4,3},{5,4},{6,5},{7,6},{8,7},{9,8},{10,9... | collective-permute-start | bytes 786440 | tf_op jit(solution)/shard_map/ppermute | solution.py:291
  57.3 3.4 %collective-permute-start.5 = (bf16[2,128,512]{2,1,0:T(8,128)(2,1)S(1)}, bf16[2,128,512]{2,1,0:T(8,128)(2,1)S(1)}, u32[]{:S(2)}, u32[]{:S(2)}) collective-permute-start(bf16[2,128,512]{2,1,0:T(8,128)(2,1)S(1)} %get-tuple-element.23), channel_id=1, source_target_pairs={{0,1},{1,2},{2,3},{3,4},{4,5},{5,6},{6,7},{7,8},{8,9},{9,10},{10,1... | collective-permute-start | bytes 786440 | tf_op jit(solution)/shard_map/ppermute | solution.py:291
  60.7 2.8 %collective-permute-done.4 = bf16[2,128,512]{2,1,0:T(8,128)(2,1)S(1)} collective-permute-done((bf16[2,128,512]{2,1,0:T(8,128)(2,1)S(1)}, bf16[2,128,512]{2,1,0:T(8,128)(2,1)S(1)}, u32[]{:S(2)}, u32[]{:S(2)}) %collective-permute-start.4) | collective-permute-done | bytes 262176 | tf_op jit(solution)/shard_map/ppermute | solution.py:291
  63.5 0.1 add.10
  63.5 5.5 %collective-permute-start.6 = (bf16[2,128,512]{2,1,0:T(8,128)(2,1)S(1)}, bf16[2,128,512]{2,1,0:T(8,128)(2,1)S(1)}, u32[]{:S(2)}, u32[]{:S(2)}) collective-permute-start(bf16[2,128,512]{2,1,0:T(8,128)(2,1)S(1)} %add.10), channel_id=1, source_target_pairs={{0,31},{1,0},{2,1},{3,2},{4,3},{5,4},{6,5},{7,6},{8,7},{9,8},{10,9... | collective-permute-start | bytes 786440 | tf_op jit(solution)/shard_map/ppermute | solution.py:291
  69.1 0.0 collective-permute-done.5
  69.1 0.0 copy-start.2
  69.1 0.1 add.11
  69.2 3.4 %collective-permute-start.7 = (bf16[2,128,512]{2,1,0:T(8,128)(2,1)S(1)}, bf16[2,128,512]{2,1,0:T(8,128)(2,1)S(1)}, u32[]{:S(2)}, u32[]{:S(2)}) collective-permute-start(bf16[2,128,512]{2,1,0:T(8,128)(2,1)S(1)} %add.11), channel_id=1, source_target_pairs={{0,28},{1,29},{2,30},{3,31},{4,0},{5,1},{6,2},{7,3},{8,4},{9,5},{1... | collective-permute-start | bytes 786440 | tf_op jit(solution)/shard_map/ppermute | solution.py:291
  72.6 0.0 copy-done.2
  72.6 16.5 %all_to_all.10.rows_ref = f32[16,1,128]{2,1,0:T(1,128)S(1)} all-to-all(f32[16,1,128]{2,1,0:T(1,128)S(1)} %copy-done.2), channel_id=1, replica_groups=mesh['dp'=16,'ctx'=32] {'dp'}, dimensions={0} | all-to-all | bytes 16384 | tf_op jit(solution)/shard_map/all_to_all | solution.py:262
  89.1 0.0 collective-permute-done.6.near_ref
  89.2 0.0 collective-permute-done.7.fourth_ref
  89.2 1.3 %gradients.1 = (bf16[128,4096]{1,0:T(8,128)(2,1)}, bf16[128,512]{1,0:T(8,128)(2,1)}, bf16[128,512]{1,0:T(8,128)(2,1)}) custom-call(f32[16,1,128]{2,1,0:T(1,128)S(1)} %all_to_all.10.rows_ref, bf16[128,4096]{1,0:T(8,128)(2,1)S(1)} %get-tuple-element.25.dq_ref, f32[2,128,512]{2,1,0:T(8,128)S(1)} %get-tuple-element.26.own_ref, ...), custom_call_target="tpu_custom_call" | custom-call | tf_op jit(solution)/shard_map/gradients/pallas_call | solution.py:246
  (1 shorter events, 0.0 us)
Async XLA Ops:
  1.7 23.7 %collective-permute-start.1 = (bf16[2,128,512]{2,1,0:T(8,128)(2,1)S(1)}, bf16[2,128,512]{2,1,0:T(8,128)(2,1)S(1)}, u32[]{:S(2)}, u32[]{:S(2)}) collective-permute-start(bf16[2,128,512]{2,1,0:T(8,128)(2,1)S(1)} %broadcast_select_fusion.own_ref), channel_id=1, source_target_pairs={{0,4},{1,5},{2,6},{3,7},{4,8},{5,9},{6,10},{7,11},{8,12},{9,13},{1... | collective-permute-start | bytes 786440 | tf_op jit(solution)/shard_map/ppermute | solution.py:291
  13.2 20.2 %collective-permute-start = (bf16[2,128,512]{2,1,0:T(8,128)(2,1)S(1)}, bf16[2,128,512]{2,1,0:T(8,128)(2,1)S(1)}, u32[]{:S(2)}, u32[]{:S(2)}) collective-permute-start(bf16[2,128,512]{2,1,0:T(8,128)(2,1)S(1)} %broadcast_select_fusion.own_ref), channel_id=1, source_target_pairs={{0,1},{1,2},{2,3},{3,4},{4,5},{5,6},{6,7},{7,8},{8,9},{9,10},{10,1... | collective-permute-start | bytes 786440 | tf_op jit(solution)/shard_map/ppermute | solution.py:291
  17.7 17.9 %all-to-all-start = ((f32[32,1,128]{2,1,0:T(1,128)}), f32[32,1,128]{2,1,0:T(1,128)S(1)}, u32[]{:S(2)}, u32[]{:S(2)}) async-start(f32[32,1,128]{2,1,0:T(1,128)} %spread_total.2), calls=%async_computation | async-start | bytes 32768 | tf_op jit(solution)/shard_map/all_to_all | solution.py:262
  23.9 0.7 copy-start.3
  24.7 0.7 copy-start.4
  25.4 13.8 %collective-permute-start.3 = (bf16[2,128,512]{2,1,0:T(8,128)(2,1)S(1)}, bf16[2,128,512]{2,1,0:T(8,128)(2,1)S(1)}, u32[]{:S(2)}, u32[]{:S(2)}) collective-permute-start(bf16[2,128,512]{2,1,0:T(8,128)(2,1)S(1)} %collective-permute-done.1.fourth_ref), channel_id=1, source_target_pairs={{0,31},{1,0},{2,1},{3,2},{4,3},{5,4},{6,5},{7,6},{8,7},{9,8},{10,9... | collective-permute-start | bytes 786440 | tf_op jit(solution)/shard_map/ppermute | solution.py:291
  33.4 12.3 %collective-permute-start.2 = (bf16[2,128,512]{2,1,0:T(8,128)(2,1)S(1)}, bf16[2,128,512]{2,1,0:T(8,128)(2,1)S(1)}, u32[]{:S(2)}, u32[]{:S(2)}) collective-permute-start(bf16[2,128,512]{2,1,0:T(8,128)(2,1)S(1)} %collective-permute-done.near_ref), channel_id=1, source_target_pairs={{0,1},{1,2},{2,3},{3,4},{4,5},{5,6},{6,7},{7,8},{8,9},{9,10},{10,1... | collective-permute-start | bytes 786440 | tf_op jit(solution)/shard_map/ppermute | solution.py:291
  35.6 0.6 copy-start.1
  37.7 8.0 %copy-start = (bf16[1,128,4096]{2,1,0:T(8,128)(2,1)S(1)}, bf16[1,128,4096]{2,1,0:T(8,128)(2,1)}, u32[]{:S(2)}) copy-start(bf16[1,128,4096]{2,1,0:T(8,128)(2,1)} %param.7) | copy-start | bytes 3145732
  55.4 8.0 %collective-permute-start.4 = (bf16[2,128,512]{2,1,0:T(8,128)(2,1)S(1)}, bf16[2,128,512]{2,1,0:T(8,128)(2,1)S(1)}, u32[]{:S(2)}, u32[]{:S(2)}) collective-permute-start(bf16[2,128,512]{2,1,0:T(8,128)(2,1)S(1)} %get-tuple-element.21), channel_id=1, source_target_pairs={{0,31},{1,0},{2,1},{3,2},{4,3},{5,4},{6,5},{7,6},{8,7},{9,8},{10,9... | collective-permute-start | bytes 786440 | tf_op jit(solution)/shard_map/ppermute | solution.py:291
  57.3 11.7 %collective-permute-start.5 = (bf16[2,128,512]{2,1,0:T(8,128)(2,1)S(1)}, bf16[2,128,512]{2,1,0:T(8,128)(2,1)S(1)}, u32[]{:S(2)}, u32[]{:S(2)}) collective-permute-start(bf16[2,128,512]{2,1,0:T(8,128)(2,1)S(1)} %get-tuple-element.23), channel_id=1, source_target_pairs={{0,1},{1,2},{2,3},{3,4},{4,5},{5,6},{6,7},{7,8},{8,9},{9,10},{10,1... | collective-permute-start | bytes 786440 | tf_op jit(solution)/shard_map/ppermute | solution.py:291
  63.5 25.6 %collective-permute-start.6 = (bf16[2,128,512]{2,1,0:T(8,128)(2,1)S(1)}, bf16[2,128,512]{2,1,0:T(8,128)(2,1)S(1)}, u32[]{:S(2)}, u32[]{:S(2)}) collective-permute-start(bf16[2,128,512]{2,1,0:T(8,128)(2,1)S(1)} %add.10), channel_id=1, source_target_pairs={{0,31},{1,0},{2,1},{3,2},{4,3},{5,4},{6,5},{7,6},{8,7},{9,8},{10,9... | collective-permute-start | bytes 786440 | tf_op jit(solution)/shard_map/ppermute | solution.py:291
  69.1 3.5 %copy-start.2 = (f32[16,1,128]{2,1,0:T(1,128)S(1)}, f32[16,1,128]{2,1,0:T(1,128)}, u32[]{:S(2)}) copy-start(f32[16,1,128]{2,1,0:T(1,128)} %spread_total.3) | copy-start | bytes 24580
  69.2 20.0 %collective-permute-start.7 = (bf16[2,128,512]{2,1,0:T(8,128)(2,1)S(1)}, bf16[2,128,512]{2,1,0:T(8,128)(2,1)S(1)}, u32[]{:S(2)}, u32[]{:S(2)}) collective-permute-start(bf16[2,128,512]{2,1,0:T(8,128)(2,1)S(1)} %add.11), channel_id=1, source_target_pairs={{0,28},{1,29},{2,30},{3,31},{4,0},{5,1},{6,2},{7,3},{8,4},{9,5},{1... | collective-permute-start | bytes 786440 | tf_op jit(solution)/shard_map/ppermute | solution.py:291
